TPU v7x, 128 devices: a whole 4x4x4 slice. The times are simulated.
128 devices in a mesh: sec: 2 (over core), gx: 8 (over x_hi, z), gy: 8 (over x_lo, y).
Axes of the slice: x: 4 (x_hi: 2, x_lo: 2; x = x_hi * 2 + x_lo), y: 4, z: 4, core: 2. Of those that a mesh axis runs over, the one named last changes fastest.
Arguments:
- slide_thickness: float32 [16, 8, 64, 1024], P(('sec', 'gy'), 'gx'), may hold values from 0.2 to 2
- footprint: int32 [16, 8, 64, 1024], P(('sec', 'gy'), 'gx'), may hold values 0 or 1
- slide_momentum: float32 [16, 8, 64, 1024], P(('sec', 'gy'), 'gx'), may hold values from -1.5 to 1.5
- bed_friction: float32 [16, 8, 64, 1024], P(('sec', 'gy'), 'gx'), may hold values from 0.1 to 1
- surface: float32 [8192, 1024], P(('sec', 'gy'), 'gx'), may hold values from -2 to 2
- flux_x: float32 [3, 8192, 1024], P(None, ('sec', 'gy'), 'gx'), may hold values from -2 to 2
- flux_y: float32 [3, 8192, 1024], P(None, ('sec', 'gy'), 'gx'), may hold values from -2 to 2
- bathy_class: int32 [8192, 1024], P(('sec', 'gy'), 'gx'), may hold values from 0 to 7
- depth_table: float32 [8], replicated, may hold values from 2 to 8
Outputs:
- surface_out: float32 [8192, 1024], P(('sec', 'gy'), 'gx')
- pressure_out: float32 [3, 8192, 1024], P(None, ('sec', 'gy'), 'gx')
- bottom_load: float32 [16, 8, 64, 1024], P(('sec', 'gy'), 'gx')
- thickness_out: float32 [1024, 8192], P(('sec', 'gx', 'gy'))
- momentum_out: float32 [1024, 8192], P(('sec', 'gx', 'gy'))
All inputs are finite; a program needn't handle non-finite values. No bound on the sum of `footprint` on one device may be relied on, other than what follows from the above.
Results may differ from a plain program's by a relative error of at most 0.0001.
Values sent between devices are 32-bit elements; how exact they have to be, the bound alone decides.
A program may use at most 128 MiB of HBM per device.

v0:
```python
import jax
import jax.numpy as jnp
from jax import lax
from jax.sharding import PartitionSpec as P

LEVELS = 4
SWEEPS = 4


SPREAD = 0.25
GRAVITY_PUSH = 0.4
SOURCE = 2.0
SURFACE_STEP = 0.2
COURANT = 0.25
SLOPE_PULL = 0.5
LAYER_SHARE = (0.2, 0.3, 0.5)


def with_halo(cells, sides, width):
    for axis, dim in sides:
        count = lax.axis_size(axis)
        ends = count - 1
        head = lax.slice_in_dim(cells, 0, width, axis=dim)
        tail = lax.slice_in_dim(cells, cells.shape[dim] - width, cells.shape[dim], axis=dim)
        cells = jnp.concatenate(
            [
                lax.ppermute(tail, axis, [(i, (i + 1) % count) for i in range(ends)]),
                cells,
                lax.ppermute(head, axis, [((i + 1) % count, i) for i in range(ends)]),
            ],
            axis=dim,
        )
    return cells


def in_one_piece(arrays, axis, split_dim, concat_dim, along):
    ends, at = ([], 0)
    for a in arrays[:-1]:
        at += a.shape[along]
        ends.append(at)
    both = jnp.concatenate(arrays, axis=along)
    return tuple(
        jnp.split(
            lax.all_to_all(both, axis, split_axis=split_dim, concat_axis=concat_dim, tiled=True),
            ends,
            axis=along,
        )
    )


def slide_step(thickness, moment, friction):
    speed = moment / (1.0 + jnp.abs(thickness))
    flux_moment = moment * speed + 0.5 * thickness * thickness

    def beside(field):
        padded = jnp.pad(field, ((0, 0), (1, 1)))
        return (padded[:, :-2], padded[:, 2:])

    thick_lo, thick_hi = beside(thickness)
    moment_lo, moment_hi = beside(moment)
    mass_lo, mass_hi = beside(moment)
    carry_lo, carry_hi = beside(flux_moment)
    new_thickness = 0.5 * (thick_lo + thick_hi) - 0.5 * COURANT * (mass_hi - mass_lo)
    drag = friction * thickness * speed / jnp.sqrt(speed * speed + 1.0)
    new_moment = (
        0.5 * (moment_lo + moment_hi)
        - 0.5 * COURANT * (carry_hi - carry_lo)
        + COURANT * (SLOPE_PULL * thickness - drag)
    )
    return (new_thickness, new_moment)


def diff_east(padded):
    return (padded[..., 1:-1, 2:] - padded[..., 1:-1, :-2]) * 0.5


def diff_north(padded):
    return (padded[..., 2:, 1:-1] - padded[..., :-2, 1:-1]) * 0.5


def neighbours(padded):
    return (
        padded[..., 1:-1, 2:]
        + padded[..., 1:-1, :-2]
        + padded[..., 2:, 1:-1]
        + padded[..., :-2, 1:-1]
    )


def lookup_depth(bathy_class, depth_table):
    water_depth = jnp.zeros(bathy_class.shape, jnp.float32)
    for class_index in range(depth_table.shape[0]):
        water_depth = water_depth + jnp.where(
            bathy_class == class_index, depth_table[class_index], 0.0
        )
    return water_depth


def vertical_inverse(water_depth):
    coupling = 9.0 / (water_depth * water_depth)
    horizontal = 4.0 * SPREAD
    diag_top = horizontal + 3.0 * coupling
    diag_mid = horizontal + 2.0 * coupling
    diag_low = horizontal + coupling
    square = coupling * coupling
    determinant = diag_top * (diag_mid * diag_low - square) - square * diag_low
    return (
        jnp.stack(
            [
                diag_mid * diag_low - square,
                coupling * diag_low,
                square,
                diag_top * diag_low,
                coupling * diag_top,
                diag_top * diag_mid - square,
            ]
        )
        / determinant
    )


def apply_inverse(inverse, vector):
    top = inverse[0] * vector[0] + inverse[1] * vector[1] + inverse[2] * vector[2]
    mid = inverse[1] * vector[0] + inverse[3] * vector[1] + inverse[4] * vector[2]
    low = inverse[2] * vector[0] + inverse[4] * vector[1] + inverse[5] * vector[2]
    return jnp.stack([top, mid, low])


def crop_cycle(field, amount):
    return field[..., amount : field.shape[-2] - amount, amount : field.shape[-1] - amount]


def shards(
    slide_thickness,
    footprint,
    slide_momentum,
    bed_friction,
    surface,
    flux_x,
    flux_y,
    bathy_class,
    depth_table,
):
    thickness = (slide_thickness * footprint.astype(jnp.float32))[0, 0]
    moment = slide_momentum[0, 0]
    friction = bed_friction[0, 0]
    strip_w, cells_x = thickness.shape
    gx_count = lax.axis_size("gx")
    sec_count = lax.axis_size("sec")
    gy_count = lax.axis_size("gy")
    tile_x = cells_x // gx_count
    tile_y = surface.shape[0]
    rises_strip = []
    for level_index in range(LEVELS):
        new_thickness, moment = slide_step(thickness, moment, friction)
        rises_strip.append(new_thickness - thickness)
        thickness = new_thickness
    stacked = jnp.stack(rises_strip).reshape(LEVELS, strip_w, gx_count, tile_x)
    moved = lax.all_to_all(stacked, "gx", split_axis=2, concat_axis=1, tiled=True).reshape(
        LEVELS, gx_count * strip_w, tile_x
    )
    rises = [moved[level_index] for level_index in range(LEVELS)]
    inverse = vertical_inverse(lookup_depth(bathy_class, depth_table))
    share = jnp.array(LAYER_SHARE, dtype=jnp.float32)[:, None, None]
    surface_now = surface
    flux_east = flux_x
    flux_north = flux_y
    pressure = jnp.zeros(flux_x.shape, jnp.float32)
    bottom_sum = jnp.zeros(surface.shape, jnp.float32)
    depth_rim = SWEEPS + 4
    inverse_wide = with_halo(inverse, ((("sec", "gy"), 1), ("gx", 2)), depth_rim)
    row_global = (
        lax.axis_index(("sec", "gy")) * tile_y + jnp.arange(tile_y + 2 * depth_rim) - depth_rim
    )
    column_global = lax.axis_index("gx") * tile_x + jnp.arange(tile_x + 2 * depth_rim) - depth_rim
    row_inside = (row_global >= 0) & (row_global < tile_y * sec_count * gy_count)
    column_inside = (column_global >= 0) & (column_global < tile_x * gx_count)
    inside_grid = (row_inside[:, None] & column_inside[None, :]).astype(jnp.float32)
    for level_index in range(LEVELS):
        wide_eta, wide_east, wide_north, wide_press, wide_rise = (
            with_halo(surface_now[None], ((("sec", "gy"), 1), ("gx", 2)), depth_rim),
            with_halo(flux_east, ((("sec", "gy"), 1), ("gx", 2)), depth_rim),
            with_halo(flux_north, ((("sec", "gy"), 1), ("gx", 2)), depth_rim),
            with_halo(pressure, ((("sec", "gy"), 1), ("gx", 2)), depth_rim),
            with_halo(rises[level_index][None], ((("sec", "gy"), 1), ("gx", 2)), depth_rim),
        )
        eta_wide = wide_eta[0]
        rise_wide = wide_rise[0]
        pred_east = (crop_cycle(wide_east, 1) - GRAVITY_PUSH * diff_east(eta_wide)) * crop_cycle(
            inside_grid, 1
        )
        pred_north = (crop_cycle(wide_north, 1) - GRAVITY_PUSH * diff_north(eta_wide)) * crop_cycle(
            inside_grid, 1
        )
        source_deep = (
            -(diff_east(pred_east) + diff_north(pred_north))
            + SOURCE * share * crop_cycle(rise_wide, 2)[None]
        )
        press_deep = crop_cycle(wide_press, 2)
        for sweep in range(SWEEPS):
            press_deep = apply_inverse(
                crop_cycle(inverse_wide, 3 + sweep),
                crop_cycle(source_deep, 1 + sweep) + SPREAD * neighbours(press_deep),
            )
        outer_mask = crop_cycle(inside_grid, SWEEPS + 3)
        corr_east = (
            crop_cycle(pred_east, SWEEPS + 2) - SPREAD * diff_east(press_deep)
        ) * outer_mask
        corr_north = (
            crop_cycle(pred_north, SWEEPS + 2) - SPREAD * diff_north(press_deep)
        ) * outer_mask
        surface_now = (
            crop_cycle(eta_wide, depth_rim)
            - SURFACE_STEP * jnp.sum(diff_east(corr_east) + diff_north(corr_north), axis=0)
            + crop_cycle(rise_wide, depth_rim)
        )
        flux_east = crop_cycle(corr_east, 1)
        flux_north = crop_cycle(corr_north, 1)
        pressure = crop_cycle(press_deep, depth_rim - SWEEPS - 2)
        bottom_sum = bottom_sum + pressure[2]
    mean_bottom = (bottom_sum / LEVELS).reshape(gx_count, strip_w, tile_x)
    returned = lax.all_to_all(mean_bottom, "gx", split_axis=0, concat_axis=2, tiled=True)
    bottom_load = returned.reshape(strip_w, cells_x)[None, None]
    device_count = sec_count * gx_count * gy_count
    row_count = cells_x // device_count

    def arrange(received):
        shaped = received.reshape(strip_w, sec_count, gx_count, gy_count, row_count)
        shaped = jnp.transpose(shaped, (1, 3, 2, 0, 4))
        return shaped.reshape(-1, row_count).T

    got_thick, got_moment = in_one_piece(
        (
            thickness.reshape(strip_w, device_count, row_count),
            moment.reshape(strip_w, device_count, row_count),
        ),
        ("sec", "gx", "gy"),
        1,
        1,
        0,
    )
    thickness_out = arrange(got_thick)
    momentum_out = arrange(got_moment)
    return (surface_now, pressure, bottom_load, thickness_out, momentum_out)


def solution(mesh):
    placed = (
        P(("sec", "gy"), "gx", None, None),
        P(("sec", "gy"), "gx", None, None),
        P(("sec", "gy"), "gx", None, None),
        P(("sec", "gy"), "gx", None, None),
        P(("sec", "gy"), "gx"),
        P(None, ("sec", "gy"), "gx"),
        P(None, ("sec", "gy"), "gx"),
        P(("sec", "gy"), "gx"),
        P(),
    )
    return jax.shard_map(
        shards,
        mesh=mesh,
        in_specs=placed,
        out_specs=(
            P(("sec", "gy"), "gx"),
            P(None, ("sec", "gy"), "gx"),
            P(("sec", "gy"), "gx", None, None),
            P(("sec", "gx", "gy"), None),
            P(("sec", "gx", "gy"), None),
        ),
        check_vma=False,
    )
```

profile of v0, /device:TPU:24, one launch (start us, length us, event | category | flops | bytes accessed | tf_op | source)
XLA Modules:
  0.0 721.1 jit_solution(7480186118841555936)
XLA Ops:
  0.7 2.8 collective-permute-start.21
  3.5 5.3 collective-permute-start.20
  11.4 6.0 collective-permute-start
  27.0 11.5 %all-to-all-start.2 = ((f32[128,128,8]{0,2,1:T(8,128)}), f32[128,128,8]{0,2,1:T(8,128)S(1)}, u32[]{:S(2)}, u32[]{:S(2)}) async-start(f32[128,128,8]{0,2,1:T(8,128)} %pad_maximum_fusion.61), calls=%async_computation.2 | async-start | bytes 1048576 | tf_op jit(solution)/shard_map/all_to_all | solution.py:44
  39.2 5.9 bitcast_dynamic-update-slice_fusion.3
  45.1 5.9 fusion.141
  54.0 5.8 fusion.138
  59.8 5.8 bitcast_dynamic-update-slice_fusion.2
  65.7 5.9 fusion.140
  71.5 5.9 bitcast_dynamic-update-slice_fusion.1
  77.4 5.9 bitcast_dynamic-update-slice_fusion
  88.3 2.7 collective-permute-start.5
  91.0 5.2 collective-permute-start.12
  102.5 6.0 collective-permute-start.8
  111.4 5.3 collective-permute-start.2
  127.1 5.2 collective-permute-start.22
  136.4 5.2 collective-permute-start.6
  143.0 5.3 collective-permute-start.14
  157.9 8.8 %collective-permute-start.10 = (f32[6,528,8]{1,2,0:T(8,128)S(1)}, f32[6,528,8]{1,2,0:T(8,128)}, u32[]{:S(2)}, u32[]{:S(2)}) collective-permute-start(f32[6,528,8]{1,2,0:T(8,128)S(1)} %copy.72), channel_id=1, source_target_pairs={{0,8},{8,16},{16,24},{24,32},{32,40},{40,48},{48,56},{1,9},{9,17},... | collective-permute-start | bytes 304136 | tf_op jit(solution)/shard_map/ppermute | solution.py:27
  174.0 16.1 %all-to-all-start = ((f32[4,64,8,128]{3,1,0,2:T(8,128)}), f32[4,64,8,128]{3,1,0,2:T(8,128)}, u32[]{:S(2)}, u32[]{:S(2)}) async-start(f32[4,64,8,128]{3,1,0,2:T(8,128)} %copy.80), calls=%async_computation | async-start | bytes 2097152 | tf_op jit(solution)/shard_map/all_to_all | solution.py:159
  190.2 5.8 fusion.39
  197.9 2.5 copy.75
  200.5 2.6 copy.74
  203.1 3.8 pad_maximum_fusion
  218.2 6.0 collective-permute-start.76
  226.2 6.0 collective-permute-start.56
  234.2 6.0 collective-permute-start.36
  242.3 6.0 collective-permute-start.16
  249.8 4.6 collective-permute-start.78
  257.2 5.2 collective-permute-start.18
  262.6 3.9 collective-permute-done.19
  266.5 3.6 collective-permute-start.58
  293.9 6.2 collective-permute-start.38
  302.4 6.0 collective-permute-start.24
  310.7 6.0 collective-permute-start.40
  322.4 6.0 collective-permute-start.28
  331.3 6.0 collective-permute-start.32
  344.4 8.9 %collective-permute-start.26 = (f32[1,528,8]{2,1,0:T(8,128)}, f32[1,528,8]{2,1,0:T(8,128)}, u32[]{:S(2)}, u32[]{:S(2)}) collective-permute-start(f32[1,528,8]{2,1,0:T(8,128)} %get-tuple-element.172), channel_id=1, source_target_pairs={{0,8},{8,16},{16,24},{24,32},{32,40},{40,48},{48,56},{1,9},{9,17},... | collective-permute-start | bytes 50696 | tf_op jit(solution)/shard_map/ppermute | solution.py:27
  363.9 5.8 collective-permute-start.30
  369.6 2.9 fusion.191
  377.9 7.6 %collective-permute-start.34 = (f32[3,528,8]{1,2,0:T(8,128)}, f32[3,528,8]{1,2,0:T(8,128)}, u32[]{:S(2)}, u32[]{:S(2)}) collective-permute-start(f32[3,528,8]{1,2,0:T(8,128)} %copy.89), channel_id=1, source_target_pairs={{0,8},{8,16},{16,24},{24,32},{32,40},{40,48},{48,56},{1,9},{9,17},... | collective-permute-start | bytes 152072 | tf_op jit(solution)/shard_map/ppermute | solution.py:27
  389.2 7.1 collective-permute-start.42
  404.3 4.7 fusion.29
  440.2 6.0 collective-permute-start.44
  448.5 6.0 collective-permute-start.60
  456.5 6.0 collective-permute-start.48
  465.4 6.0 collective-permute-start.52
  476.4 8.9 %collective-permute-start.46 = (f32[1,528,8]{2,1,0:T(8,128)}, f32[1,528,8]{2,1,0:T(8,128)}, u32[]{:S(2)}, u32[]{:S(2)}) collective-permute-start(f32[1,528,8]{2,1,0:T(8,128)} %get-tuple-element.170), channel_id=1, source_target_pairs={{0,8},{8,16},{16,24},{24,32},{32,40},{40,48},{48,56},{1,9},{9,17},... | collective-permute-start | bytes 50696 | tf_op jit(solution)/shard_map/ppermute | solution.py:27
  496.8 8.7 %collective-permute-start.50 = (f32[3,528,8]{1,2,0:T(8,128)}, f32[3,528,8]{1,2,0:T(8,128)}, u32[]{:S(2)}, u32[]{:S(2)}) collective-permute-start(f32[3,528,8]{1,2,0:T(8,128)} %copy.97), channel_id=1, source_target_pairs={{0,8},{8,16},{16,24},{24,32},{32,40},{40,48},{48,56},{1,9},{9,17},... | collective-permute-start | bytes 152072 | tf_op jit(solution)/shard_map/ppermute | solution.py:27
  513.6 5.2 collective-permute-start.54
  522.4 4.5 collective-permute-start.62
  535.1 4.7 fusion.19
  570.9 6.0 collective-permute-start.64
  579.3 6.0 collective-permute-start.80
  587.3 6.0 collective-permute-start.68
  596.1 6.0 collective-permute-start.72
  607.1 8.9 %collective-permute-start.66 = (f32[1,528,8]{2,1,0:T(8,128)}, f32[1,528,8]{2,1,0:T(8,128)}, u32[]{:S(2)}, u32[]{:S(2)}) collective-permute-start(f32[1,528,8]{2,1,0:T(8,128)} %get-tuple-element.168), channel_id=1, source_target_pairs={{0,8},{8,16},{16,24},{24,32},{32,40},{40,48},{48,56},{1,9},{9,17},... | collective-permute-start | bytes 50696 | tf_op jit(solution)/shard_map/ppermute | solution.py:27
  627.4 8.7 %collective-permute-start.70 = (f32[3,528,8]{1,2,0:T(8,128)}, f32[3,528,8]{1,2,0:T(8,128)}, u32[]{:S(2)}, u32[]{:S(2)}) collective-permute-start(f32[3,528,8]{1,2,0:T(8,128)} %copy.109), channel_id=1, source_target_pairs={{0,8},{8,16},{16,24},{24,32},{32,40},{40,48},{48,56},{1,9},{9,17},... | collective-permute-start | bytes 152072 | tf_op jit(solution)/shard_map/ppermute | solution.py:27
  644.2 5.2 collective-permute-start.74
  652.2 4.5 collective-permute-start.82
  664.8 4.7 fusion.9
  691.0 3.9 fusion.45
  698.6 12.6 %all-to-all-start.1 = ((f32[8,64,128]{2,1,0:T(8,128)}), f32[8,64,128]{2,1,0:T(8,128)S(1)}, u32[]{:S(2)}, u32[]{:S(2)}) async-start(f32[8,64,128]{2,1,0:T(8,128)} %bitcast.36), calls=%async_computation.1 | async-start | bytes 524288 | tf_op jit(solution)/shard_map/all_to_all | solution.py:222
  714.1 5.9 all-to-all-done.1
  (555 shorter events, 333.4 us)
Async XLA Ops:
  0.7 96.4 %collective-permute-start.21 = (f32[3,8,128]{2,1,0:T(8,128)S(1)}, f32[3,8,128]{2,1,0:T(8,128)S(1)}, u32[]{:S(2)}, u32[]{:S(2)}) collective-permute-start(f32[3,8,128]{2,1,0:T(8,128)S(1)} %broadcast.154), channel_id=1, source_target_pairs={{1,0},{2,1},{3,2},{4,3},{5,4},{6,5},{7,6},{64,7},{65,64},{66,65},{... | collective-permute-start | bytes 36872 | tf_op jit(solution)/shard_map/ppermute | solution.py:29
  3.5 95.5 %collective-permute-start.20 = (f32[3,8,128]{2,1,0:T(8,128)S(1)}, f32[3,8,128]{2,1,0:T(8,128)S(1)}, u32[]{:S(2)}, u32[]{:S(2)}) collective-permute-start(f32[3,8,128]{2,1,0:T(8,128)S(1)} %broadcast.154), channel_id=1, source_target_pairs={{0,1},{1,2},{2,3},{3,4},{4,5},{5,6},{6,7},{7,64},{64,65},{65,66},{... | collective-permute-start | bytes 36872 | tf_op jit(solution)/shard_map/ppermute | solution.py:27
  9.5 78.8 %collective-permute-start.1 = (f32[1,8,128]{2,1,0:T(8,128)S(1)}, f32[1,8,128]{2,1,0:T(8,128)S(1)}, u32[]{:S(2)}, u32[]{:S(2)}) collective-permute-start(f32[1,8,128]{2,1,0:T(8,128)S(1)} %get-tuple-element.191), channel_id=1, source_target_pairs={{1,0},{2,1},{3,2},{4,3},{5,4},{6,5},{7,6},{64,7},{65,64},{66,65},{... | collective-permute-start | bytes 12296 | tf_op jit(solution)/shard_map/ppermute | solution.py:29
  11.4 79.6 %collective-permute-start = (f32[1,8,128]{2,1,0:T(8,128)S(1)}, f32[1,8,128]{2,1,0:T(8,128)S(1)}, u32[]{:S(2)}, u32[]{:S(2)}) collective-permute-start(f32[1,8,128]{2,1,0:T(8,128)S(1)} %get-tuple-element.190), channel_id=1, source_target_pairs={{0,1},{1,2},{2,3},{3,4},{4,5},{5,6},{6,7},{7,64},{64,65},{65,66},{... | collective-permute-start | bytes 12296 | tf_op jit(solution)/shard_map/ppermute | solution.py:27
  18.8 83.7 %collective-permute-start.4 = (f32[3,8,128]{2,1,0:T(8,128)S(1)}, f32[3,8,128]{2,1,0:T(8,128)S(1)}, u32[]{:S(2)}, u32[]{:S(2)}) collective-permute-start(f32[3,8,128]{2,1,0:T(8,128)S(1)} %get-tuple-element.146), channel_id=1, source_target_pairs={{0,1},{1,2},{2,3},{3,4},{4,5},{5,6},{6,7},{7,64},{64,65},{65,66},{... | collective-permute-start | bytes 36872 | tf_op jit(solution)/shard_map/ppermute | solution.py:27
  27.0 147.0 %all-to-all-start.2 = ((f32[128,128,8]{0,2,1:T(8,128)}), f32[128,128,8]{0,2,1:T(8,128)S(1)}, u32[]{:S(2)}, u32[]{:S(2)}) async-start(f32[128,128,8]{0,2,1:T(8,128)} %pad_maximum_fusion.61), calls=%async_computation.2 | async-start | bytes 1048576 | tf_op jit(solution)/shard_map/all_to_all | solution.py:44
  99.0 37.5 %collective-permute-start.9 = (f32[6,8,128]{2,1,0:T(8,128)}, f32[6,8,128]{2,1,0:T(8,128)S(1)}, u32[]{:S(2)}, u32[]{:S(2)}) collective-permute-start(f32[6,8,128]{2,1,0:T(8,128)} %get-tuple-element.116), channel_id=1, source_target_pairs={{1,0},{2,1},{3,2},{4,3},{5,4},{6,5},{7,6},{64,7},{65,64},{66,65},{... | collective-permute-start | bytes 73736 | tf_op jit(solution)/shard_map/ppermute | solution.py:29
  102.5 39.1 %collective-permute-start.8 = (f32[6,8,128]{2,1,0:T(8,128)}, f32[6,8,128]{2,1,0:T(8,128)S(1)}, u32[]{:S(2)}, u32[]{:S(2)}) collective-permute-start(f32[6,8,128]{2,1,0:T(8,128)} %get-tuple-element.115), channel_id=1, source_target_pairs={{0,1},{1,2},{2,3},{3,4},{4,5},{5,6},{6,7},{7,64},{64,65},{65,66},{... | collective-permute-start | bytes 73736 | tf_op jit(solution)/shard_map/ppermute | solution.py:27
  117.7 25.4 %collective-permute-start.23 = (f32[3,528,8]{1,2,0:T(8,128)}, f32[3,528,8]{1,2,0:T(8,128)}, u32[]{:S(2)}, u32[]{:S(2)}) collective-permute-start(f32[3,528,8]{1,2,0:T(8,128)} %copy.82), channel_id=1, source_target_pairs={{8,0},{16,8},{24,16},{32,24},{40,32},{48,40},{56,48},{9,1},{17,9},... | collective-permute-start | bytes 152072 | tf_op jit(solution)/shard_map/ppermute | solution.py:29
  127.1 27.5 %collective-permute-start.22 = (f32[3,528,8]{1,2,0:T(8,128)}, f32[3,528,8]{1,2,0:T(8,128)}, u32[]{:S(2)}, u32[]{:S(2)}) collective-permute-start(f32[3,528,8]{1,2,0:T(8,128)} %copy.81), channel_id=1, source_target_pairs={{0,8},{8,16},{16,24},{24,32},{32,40},{40,48},{48,56},{1,9},{9,17},... | collective-permute-start | bytes 152072 | tf_op jit(solution)/shard_map/ppermute | solution.py:27
  132.3 25.6 %collective-permute-start.7 = (f32[3,528,8]{1,2,0:T(8,128)}, f32[3,528,8]{1,2,0:T(8,128)}, u32[]{:S(2)}, u32[]{:S(2)}) collective-permute-start(f32[3,528,8]{1,2,0:T(8,128)} %copy.69), channel_id=1, source_target_pairs={{8,0},{16,8},{24,16},{32,24},{40,32},{48,40},{56,48},{9,1},{17,9},... | collective-permute-start | bytes 152072 | tf_op jit(solution)/shard_map/ppermute | solution.py:29
  136.4 32.3 %collective-permute-start.6 = (f32[3,528,8]{1,2,0:T(8,128)}, f32[3,528,8]{1,2,0:T(8,128)}, u32[]{:S(2)}, u32[]{:S(2)}) collective-permute-start(f32[3,528,8]{1,2,0:T(8,128)} %copy.68), channel_id=1, source_target_pairs={{0,8},{8,16},{16,24},{24,32},{32,40},{40,48},{48,56},{1,9},{9,17},... | collective-permute-start | bytes 152072 | tf_op jit(solution)/shard_map/ppermute | solution.py:27
  141.6 29.1 %collective-permute-start.15 = (f32[3,528,8]{1,2,0:T(8,128)}, f32[3,528,8]{1,2,0:T(8,128)}, u32[]{:S(2)}, u32[]{:S(2)}) collective-permute-start(f32[3,528,8]{1,2,0:T(8,128)} %copy.77), channel_id=1, source_target_pairs={{8,0},{16,8},{24,16},{32,24},{40,32},{48,40},{56,48},{9,1},{17,9},... | collective-permute-start | bytes 152072 | tf_op jit(solution)/shard_map/ppermute | solution.py:29
  143.0 29.7 %collective-permute-start.14 = (f32[3,528,8]{1,2,0:T(8,128)S(1)}, f32[3,528,8]{1,2,0:T(8,128)S(1)}, u32[]{:S(2)}, u32[]{:S(2)}) collective-permute-start(f32[3,528,8]{1,2,0:T(8,128)S(1)} %copy.76), channel_id=1, source_target_pairs={{0,8},{8,16},{16,24},{24,32},{32,40},{40,48},{48,56},{1,9},{9,17},... | collective-permute-start | bytes 152072 | tf_op jit(solution)/shard_map/ppermute | solution.py:27
  154.6 43.3 %collective-permute-start.11 = (f32[6,528,8]{1,2,0:T(8,128)S(1)}, f32[6,528,8]{1,2,0:T(8,128)}, u32[]{:S(2)}, u32[]{:S(2)}) collective-permute-start(f32[6,528,8]{1,2,0:T(8,128)S(1)} %copy.73), channel_id=1, source_target_pairs={{8,0},{16,8},{24,16},{32,24},{40,32},{48,40},{56,48},{9,1},{17,9},... | collective-permute-start | bytes 304136 | tf_op jit(solution)/shard_map/ppermute | solution.py:29
  157.9 42.6 %collective-permute-start.10 = (f32[6,528,8]{1,2,0:T(8,128)S(1)}, f32[6,528,8]{1,2,0:T(8,128)}, u32[]{:S(2)}, u32[]{:S(2)}) collective-permute-start(f32[6,528,8]{1,2,0:T(8,128)S(1)} %copy.72), channel_id=1, source_target_pairs={{0,8},{8,16},{16,24},{24,32},{32,40},{40,48},{48,56},{1,9},{9,17},... | collective-permute-start | bytes 304136 | tf_op jit(solution)/shard_map/ppermute | solution.py:27
  174.0 41.0 %all-to-all-start = ((f32[4,64,8,128]{3,1,0,2:T(8,128)}), f32[4,64,8,128]{3,1,0,2:T(8,128)}, u32[]{:S(2)}, u32[]{:S(2)}) async-start(f32[4,64,8,128]{3,1,0,2:T(8,128)} %copy.80), calls=%async_computation | async-start | bytes 2097152 | tf_op jit(solution)/shard_map/all_to_all | solution.py:159
  218.2 22.0 %collective-permute-start.76 = (f32[1,8,128]{2,1,0:T(8,128)S(1)}, f32[1,8,128]{2,1,0:T(8,128)S(1)}, u32[]{:S(2)}, u32[]{:S(2)}) collective-permute-start(f32[1,8,128]{2,1,0:T(8,128)S(1)} %get-tuple-element.198), channel_id=1, source_target_pairs={{0,1},{1,2},{2,3},{3,4},{4,5},{5,6},{6,7},{7,64},{64,65},{65,66},{... | collective-permute-start | bytes 12296 | tf_op jit(solution)/shard_map/ppermute | solution.py:27
  226.2 22.2 %collective-permute-start.56 = (f32[1,8,128]{2,1,0:T(8,128)S(1)}, f32[1,8,128]{2,1,0:T(8,128)S(1)}, u32[]{:S(2)}, u32[]{:S(2)}) collective-permute-start(f32[1,8,128]{2,1,0:T(8,128)S(1)} %get-tuple-element.196), channel_id=1, source_target_pairs={{0,1},{1,2},{2,3},{3,4},{4,5},{5,6},{6,7},{7,64},{64,65},{65,66},{... | collective-permute-start | bytes 12296 | tf_op jit(solution)/shard_map/ppermute | solution.py:27
  232.2 23.7 %collective-permute-start.37 = (f32[1,8,128]{2,1,0:T(8,128)S(1)}, f32[1,8,128]{2,1,0:T(8,128)S(1)}, u32[]{:S(2)}, u32[]{:S(2)}) collective-permute-start(f32[1,8,128]{2,1,0:T(8,128)S(1)} %get-tuple-element.195), channel_id=1, source_target_pairs={{1,0},{2,1},{3,2},{4,3},{5,4},{6,5},{7,6},{64,7},{65,64},{66,65},{... | collective-permute-start | bytes 12296 | tf_op jit(solution)/shard_map/ppermute | solution.py:29
  234.2 23.0 %collective-permute-start.36 = (f32[1,8,128]{2,1,0:T(8,128)S(1)}, f32[1,8,128]{2,1,0:T(8,128)S(1)}, u32[]{:S(2)}, u32[]{:S(2)}) collective-permute-start(f32[1,8,128]{2,1,0:T(8,128)S(1)} %get-tuple-element.194), channel_id=1, source_target_pairs={{0,1},{1,2},{2,3},{3,4},{4,5},{5,6},{6,7},{7,64},{64,65},{65,66},{... | collective-permute-start | bytes 12296 | tf_op jit(solution)/shard_map/ppermute | solution.py:27
  248.4 45.5 %collective-permute-start.79 = (f32[1,528,8]{2,1,0:T(8,128)S(1)}, f32[1,528,8]{2,1,0:T(8,128)S(1)}, u32[]{:S(2)}, u32[]{:S(2)}) collective-permute-start(f32[1,528,8]{2,1,0:T(8,128)S(1)} %get-tuple-element.183), channel_id=1, source_target_pairs={{8,0},{16,8},{24,16},{32,24},{40,32},{48,40},{56,48},{9,1},{17,9},... | collective-permute-start | bytes 50696 | tf_op jit(solution)/shard_map/ppermute | solution.py:29
  249.8 50.3 %collective-permute-start.78 = (f32[1,528,8]{2,1,0:T(8,128)S(1)}, f32[1,528,8]{2,1,0:T(8,128)S(1)}, u32[]{:S(2)}, u32[]{:S(2)}) collective-permute-start(f32[1,528,8]{2,1,0:T(8,128)S(1)} %get-tuple-element.182), channel_id=1, source_target_pairs={{0,8},{8,16},{16,24},{24,32},{32,40},{40,48},{48,56},{1,9},{9,17},... | collective-permute-start | bytes 50696 | tf_op jit(solution)/shard_map/ppermute | solution.py:27
  254.4 48.0 %collective-permute-start.59 = (f32[1,528,8]{2,1,0:T(8,128)S(1)}, f32[1,528,8]{2,1,0:T(8,128)S(1)}, u32[]{:S(2)}, u32[]{:S(2)}) collective-permute-start(f32[1,528,8]{2,1,0:T(8,128)S(1)} %get-tuple-element.181), channel_id=1, source_target_pairs={{8,0},{16,8},{24,16},{32,24},{40,32},{48,40},{56,48},{9,1},{17,9},... | collective-permute-start | bytes 50696 | tf_op jit(solution)/shard_map/ppermute | solution.py:29
  266.5 41.9 %collective-permute-start.58 = (f32[1,528,8]{2,1,0:T(8,128)S(1)}, f32[1,528,8]{2,1,0:T(8,128)S(1)}, u32[]{:S(2)}, u32[]{:S(2)}) collective-permute-start(f32[1,528,8]{2,1,0:T(8,128)S(1)} %get-tuple-element.180), channel_id=1, source_target_pairs={{0,8},{8,16},{16,24},{24,32},{32,40},{40,48},{48,56},{1,9},{9,17},... | collective-permute-start | bytes 50696 | tf_op jit(solution)/shard_map/ppermute | solution.py:27
  270.2 40.5 %collective-permute-start.39 = (f32[1,528,8]{2,1,0:T(8,128)S(1)}, f32[1,528,8]{2,1,0:T(8,128)S(1)}, u32[]{:S(2)}, u32[]{:S(2)}) collective-permute-start(f32[1,528,8]{2,1,0:T(8,128)S(1)} %get-tuple-element.179), channel_id=1, source_target_pairs={{8,0},{16,8},{24,16},{32,24},{40,32},{48,40},{56,48},{9,1},{17,9},... | collective-permute-start | bytes 50696 | tf_op jit(solution)/shard_map/ppermute | solution.py:29
  293.9 22.8 %collective-permute-start.38 = (f32[1,528,8]{2,1,0:T(8,128)S(1)}, f32[1,528,8]{2,1,0:T(8,128)S(1)}, u32[]{:S(2)}, u32[]{:S(2)}) collective-permute-start(f32[1,528,8]{2,1,0:T(8,128)S(1)} %get-tuple-element.178), channel_id=1, source_target_pairs={{0,8},{8,16},{16,24},{24,32},{32,40},{40,48},{48,56},{1,9},{9,17},... | collective-permute-start | bytes 50696 | tf_op jit(solution)/shard_map/ppermute | solution.py:27
  300.1 22.3 %collective-permute-start.25 = (f32[1,8,128]{2,1,0:T(8,128)S(1)}, f32[1,8,128]{2,1,0:T(8,128)S(1)}, u32[]{:S(2)}, u32[]{:S(2)}) collective-permute-start(f32[1,8,128]{2,1,0:T(8,128)S(1)} %get-tuple-element.189), channel_id=1, source_target_pairs={{1,0},{2,1},{3,2},{4,3},{5,4},{6,5},{7,6},{64,7},{65,64},{66,65},{... | collective-permute-start | bytes 12296 | tf_op jit(solution)/shard_map/ppermute | solution.py:29
  302.4 26.0 %collective-permute-start.24 = (f32[1,8,128]{2,1,0:T(8,128)S(1)}, f32[1,8,128]{2,1,0:T(8,128)S(1)}, u32[]{:S(2)}, u32[]{:S(2)}) collective-permute-start(f32[1,8,128]{2,1,0:T(8,128)S(1)} %get-tuple-element.188), channel_id=1, source_target_pairs={{0,1},{1,2},{2,3},{3,4},{4,5},{5,6},{6,7},{7,64},{64,65},{65,66},{... | collective-permute-start | bytes 12296 | tf_op jit(solution)/shard_map/ppermute | solution.py:27
  308.5 22.8 %collective-permute-start.41 = (f32[3,8,128]{2,1,0:T(8,128)S(1)}, f32[3,8,128]{2,1,0:T(8,128)S(1)}, u32[]{:S(2)}, u32[]{:S(2)}) collective-permute-start(f32[3,8,128]{2,1,0:T(8,128)S(1)} %get-tuple-element.114), channel_id=1, source_target_pairs={{1,0},{2,1},{3,2},{4,3},{5,4},{6,5},{7,6},{64,7},{65,64},{66,65},{... | collective-permute-start | bytes 36872 | tf_op jit(solution)/shard_map/ppermute | solution.py:29
  310.7 26.6 %collective-permute-start.40 = (f32[3,8,128]{2,1,0:T(8,128)S(1)}, f32[3,8,128]{2,1,0:T(8,128)S(1)}, u32[]{:S(2)}, u32[]{:S(2)}) collective-permute-start(f32[3,8,128]{2,1,0:T(8,128)S(1)} %get-tuple-element.113), channel_id=1, source_target_pairs={{0,1},{1,2},{2,3},{3,4},{4,5},{5,6},{6,7},{7,64},{64,65},{65,66},{... | collective-permute-start | bytes 36872 | tf_op jit(solution)/shard_map/ppermute | solution.py:27
  316.7 27.7 %collective-permute-start.29 = (f32[3,8,128]{2,1,0:T(8,128)}, f32[3,8,128]{2,1,0:T(8,128)S(1)}, u32[]{:S(2)}, u32[]{:S(2)}) collective-permute-start(f32[3,8,128]{2,1,0:T(8,128)} %get-tuple-element.107), channel_id=1, source_target_pairs={{1,0},{2,1},{3,2},{4,3},{5,4},{6,5},{7,6},{64,7},{65,64},{66,65},{... | collective-permute-start | bytes 36872 | tf_op jit(solution)/shard_map/ppermute | solution.py:29
  322.4 30.8 %collective-permute-start.28 = (f32[3,8,128]{2,1,0:T(8,128)}, f32[3,8,128]{2,1,0:T(8,128)S(1)}, u32[]{:S(2)}, u32[]{:S(2)}) collective-permute-start(f32[3,8,128]{2,1,0:T(8,128)} %get-tuple-element.106), channel_id=1, source_target_pairs={{0,1},{1,2},{2,3},{3,4},{4,5},{5,6},{6,7},{7,64},{64,65},{65,66},{... | collective-permute-start | bytes 36872 | tf_op jit(solution)/shard_map/ppermute | solution.py:27
  328.5 26.1 %collective-permute-start.33 = (f32[3,8,128]{2,1,0:T(8,128)}, f32[3,8,128]{2,1,0:T(8,128)S(1)}, u32[]{:S(2)}, u32[]{:S(2)}) collective-permute-start(f32[3,8,128]{2,1,0:T(8,128)} %get-tuple-element.112), channel_id=1, source_target_pairs={{1,0},{2,1},{3,2},{4,3},{5,4},{6,5},{7,6},{64,7},{65,64},{66,65},{... | collective-permute-start | bytes 36872 | tf_op jit(solution)/shard_map/ppermute | solution.py:29
  331.3 23.3 %collective-permute-start.32 = (f32[3,8,128]{2,1,0:T(8,128)}, f32[3,8,128]{2,1,0:T(8,128)S(1)}, u32[]{:S(2)}, u32[]{:S(2)}) collective-permute-start(f32[3,8,128]{2,1,0:T(8,128)} %get-tuple-element.111), channel_id=1, source_target_pairs={{0,1},{1,2},{2,3},{3,4},{4,5},{5,6},{6,7},{7,64},{64,65},{65,66},{... | collective-permute-start | bytes 36872 | tf_op jit(solution)/shard_map/ppermute | solution.py:27
  337.3 39.3 %collective-permute-start.27 = (f32[1,528,8]{2,1,0:T(8,128)}, f32[1,528,8]{2,1,0:T(8,128)}, u32[]{:S(2)}, u32[]{:S(2)}) collective-permute-start(f32[1,528,8]{2,1,0:T(8,128)} %get-tuple-element.173), channel_id=1, source_target_pairs={{8,0},{16,8},{24,16},{32,24},{40,32},{48,40},{56,48},{9,1},{17,9},... | collective-permute-start | bytes 50696 | tf_op jit(solution)/shard_map/ppermute | solution.py:29
  344.4 33.5 %collective-permute-start.26 = (f32[1,528,8]{2,1,0:T(8,128)}, f32[1,528,8]{2,1,0:T(8,128)}, u32[]{:S(2)}, u32[]{:S(2)}) collective-permute-start(f32[1,528,8]{2,1,0:T(8,128)} %get-tuple-element.172), channel_id=1, source_target_pairs={{0,8},{8,16},{16,24},{24,32},{32,40},{40,48},{48,56},{1,9},{9,17},... | collective-permute-start | bytes 50696 | tf_op jit(solution)/shard_map/ppermute | solution.py:27
  353.3 58.3 %collective-permute-start.43 = (f32[3,528,8]{1,2,0:T(8,128)}, f32[3,528,8]{1,2,0:T(8,128)}, u32[]{:S(2)}, u32[]{:S(2)}) collective-permute-start(f32[3,528,8]{1,2,0:T(8,128)} %copy.94), channel_id=1, source_target_pairs={{8,0},{16,8},{24,16},{32,24},{40,32},{48,40},{56,48},{9,1},{17,9},... | collective-permute-start | bytes 152072 | tf_op jit(solution)/shard_map/ppermute | solution.py:29
  360.5 28.7 %collective-permute-start.31 = (f32[3,528,8]{1,2,0:T(8,128)}, f32[3,528,8]{1,2,0:T(8,128)}, u32[]{:S(2)}, u32[]{:S(2)}) collective-permute-start(f32[3,528,8]{1,2,0:T(8,128)} %copy.86), channel_id=1, source_target_pairs={{8,0},{16,8},{24,16},{32,24},{40,32},{48,40},{56,48},{9,1},{17,9},... | collective-permute-start | bytes 152072 | tf_op jit(solution)/shard_map/ppermute | solution.py:29
  363.9 34.4 %collective-permute-start.30 = (f32[3,528,8]{1,2,0:T(8,128)}, f32[3,528,8]{1,2,0:T(8,128)}, u32[]{:S(2)}, u32[]{:S(2)}) collective-permute-start(f32[3,528,8]{1,2,0:T(8,128)} %copy.85), channel_id=1, source_target_pairs={{0,8},{8,16},{16,24},{24,32},{32,40},{40,48},{48,56},{1,9},{9,17},... | collective-permute-start | bytes 152072 | tf_op jit(solution)/shard_map/ppermute | solution.py:27
  376.6 23.7 %collective-permute-start.35 = (f32[3,528,8]{1,2,0:T(8,128)}, f32[3,528,8]{1,2,0:T(8,128)}, u32[]{:S(2)}, u32[]{:S(2)}) collective-permute-start(f32[3,528,8]{1,2,0:T(8,128)} %copy.90), channel_id=1, source_target_pairs={{8,0},{16,8},{24,16},{32,24},{40,32},{48,40},{56,48},{9,1},{17,9},... | collective-permute-start | bytes 152072 | tf_op jit(solution)/shard_map/ppermute | solution.py:29
  377.9 24.4 %collective-permute-start.34 = (f32[3,528,8]{1,2,0:T(8,128)}, f32[3,528,8]{1,2,0:T(8,128)}, u32[]{:S(2)}, u32[]{:S(2)}) collective-permute-start(f32[3,528,8]{1,2,0:T(8,128)} %copy.89), channel_id=1, source_target_pairs={{0,8},{8,16},{16,24},{24,32},{32,40},{40,48},{48,56},{1,9},{9,17},... | collective-permute-start | bytes 152072 | tf_op jit(solution)/shard_map/ppermute | solution.py:27
  389.2 24.4 %collective-permute-start.42 = (f32[3,528,8]{1,2,0:T(8,128)S(1)}, f32[3,528,8]{1,2,0:T(8,128)S(1)}, u32[]{:S(2)}, u32[]{:S(2)}) collective-permute-start(f32[3,528,8]{1,2,0:T(8,128)S(1)} %copy-done.65), channel_id=1, source_target_pairs={{0,8},{8,16},{16,24},{24,32},{32,40},{40,48},{48,56},{1,9},{9,17},... | collective-permute-start | bytes 152072 | tf_op jit(solution)/shard_map/ppermute | solution.py:27
  440.2 22.4 %collective-permute-start.44 = (f32[1,8,128]{2,1,0:T(8,128)S(1)}, f32[1,8,128]{2,1,0:T(8,128)S(1)}, u32[]{:S(2)}, u32[]{:S(2)}) collective-permute-start(f32[1,8,128]{2,1,0:T(8,128)S(1)} %get-tuple-element.186), channel_id=1, source_target_pairs={{0,1},{1,2},{2,3},{3,4},{4,5},{5,6},{6,7},{7,64},{64,65},{65,66},{... | collective-permute-start | bytes 12296 | tf_op jit(solution)/shard_map/ppermute | solution.py:27
  448.5 22.9 %collective-permute-start.60 = (f32[3,8,128]{2,1,0:T(8,128)S(1)}, f32[3,8,128]{2,1,0:T(8,128)S(1)}, u32[]{:S(2)}, u32[]{:S(2)}) collective-permute-start(f32[3,8,128]{2,1,0:T(8,128)S(1)} %get-tuple-element.104), channel_id=1, source_target_pairs={{0,1},{1,2},{2,3},{3,4},{4,5},{5,6},{6,7},{7,64},{64,65},{65,66},{... | collective-permute-start | bytes 36872 | tf_op jit(solution)/shard_map/ppermute | solution.py:27
  456.5 28.8 %collective-permute-start.48 = (f32[3,8,128]{2,1,0:T(8,128)}, f32[3,8,128]{2,1,0:T(8,128)S(1)}, u32[]{:S(2)}, u32[]{:S(2)}) collective-permute-start(f32[3,8,128]{2,1,0:T(8,128)} %get-tuple-element.97), channel_id=1, source_target_pairs={{0,1},{1,2},{2,3},{3,4},{4,5},{5,6},{6,7},{7,64},{64,65},{65,66},{... | collective-permute-start | bytes 36872 | tf_op jit(solution)/shard_map/ppermute | solution.py:27
  462.6 32.9 %collective-permute-start.53 = (f32[3,8,128]{2,1,0:T(8,128)}, f32[3,8,128]{2,1,0:T(8,128)S(1)}, u32[]{:S(2)}, u32[]{:S(2)}) collective-permute-start(f32[3,8,128]{2,1,0:T(8,128)} %get-tuple-element.103), channel_id=1, source_target_pairs={{1,0},{2,1},{3,2},{4,3},{5,4},{6,5},{7,6},{64,7},{65,64},{66,65},{... | collective-permute-start | bytes 36872 | tf_op jit(solution)/shard_map/ppermute | solution.py:29
  465.4 31.4 %collective-permute-start.52 = (f32[3,8,128]{2,1,0:T(8,128)}, f32[3,8,128]{2,1,0:T(8,128)S(1)}, u32[]{:S(2)}, u32[]{:S(2)}) collective-permute-start(f32[3,8,128]{2,1,0:T(8,128)} %get-tuple-element.102), channel_id=1, source_target_pairs={{0,1},{1,2},{2,3},{3,4},{4,5},{5,6},{6,7},{7,64},{64,65},{65,66},{... | collective-permute-start | bytes 36872 | tf_op jit(solution)/shard_map/ppermute | solution.py:27
  471.5 40.9 %collective-permute-start.47 = (f32[1,528,8]{2,1,0:T(8,128)}, f32[1,528,8]{2,1,0:T(8,128)}, u32[]{:S(2)}, u32[]{:S(2)}) collective-permute-start(f32[1,528,8]{2,1,0:T(8,128)} %get-tuple-element.171), channel_id=1, source_target_pairs={{8,0},{16,8},{24,16},{32,24},{40,32},{48,40},{56,48},{9,1},{17,9},... | collective-permute-start | bytes 50696 | tf_op jit(solution)/shard_map/ppermute | solution.py:29
  476.4 37.2 %collective-permute-start.46 = (f32[1,528,8]{2,1,0:T(8,128)}, f32[1,528,8]{2,1,0:T(8,128)}, u32[]{:S(2)}, u32[]{:S(2)}) collective-permute-start(f32[1,528,8]{2,1,0:T(8,128)} %get-tuple-element.170), channel_id=1, source_target_pairs={{0,8},{8,16},{16,24},{24,32},{32,40},{40,48},{48,56},{1,9},{9,17},... | collective-permute-start | bytes 50696 | tf_op jit(solution)/shard_map/ppermute | solution.py:27
  485.3 57.0 %collective-permute-start.63 = (f32[3,528,8]{1,2,0:T(8,128)}, f32[3,528,8]{1,2,0:T(8,128)}, u32[]{:S(2)}, u32[]{:S(2)}) collective-permute-start(f32[3,528,8]{1,2,0:T(8,128)} %copy.106), channel_id=1, source_target_pairs={{8,0},{16,8},{24,16},{32,24},{40,32},{48,40},{56,48},{9,1},{17,9},... | collective-permute-start | bytes 152072 | tf_op jit(solution)/shard_map/ppermute | solution.py:29
  495.5 27.0 %collective-permute-start.51 = (f32[3,528,8]{1,2,0:T(8,128)}, f32[3,528,8]{1,2,0:T(8,128)}, u32[]{:S(2)}, u32[]{:S(2)}) collective-permute-start(f32[3,528,8]{1,2,0:T(8,128)} %copy.98), channel_id=1, source_target_pairs={{8,0},{16,8},{24,16},{32,24},{40,32},{48,40},{56,48},{9,1},{17,9},... | collective-permute-start | bytes 152072 | tf_op jit(solution)/shard_map/ppermute | solution.py:29
  496.8 32.3 %collective-permute-start.50 = (f32[3,528,8]{1,2,0:T(8,128)}, f32[3,528,8]{1,2,0:T(8,128)}, u32[]{:S(2)}, u32[]{:S(2)}) collective-permute-start(f32[3,528,8]{1,2,0:T(8,128)} %copy.97), channel_id=1, source_target_pairs={{0,8},{8,16},{16,24},{24,32},{32,40},{40,48},{48,56},{1,9},{9,17},... | collective-permute-start | bytes 152072 | tf_op jit(solution)/shard_map/ppermute | solution.py:27
  522.4 21.9 %collective-permute-start.62 = (f32[3,528,8]{1,2,0:T(8,128)S(1)}, f32[3,528,8]{1,2,0:T(8,128)S(1)}, u32[]{:S(2)}, u32[]{:S(2)}) collective-permute-start(f32[3,528,8]{1,2,0:T(8,128)S(1)} %copy-done.67), channel_id=1, source_target_pairs={{0,8},{8,16},{16,24},{24,32},{32,40},{40,48},{48,56},{1,9},{9,17},... | collective-permute-start | bytes 152072 | tf_op jit(solution)/shard_map/ppermute | solution.py:27
  570.9 22.4 %collective-permute-start.64 = (f32[1,8,128]{2,1,0:T(8,128)S(1)}, f32[1,8,128]{2,1,0:T(8,128)S(1)}, u32[]{:S(2)}, u32[]{:S(2)}) collective-permute-start(f32[1,8,128]{2,1,0:T(8,128)S(1)} %get-tuple-element.184), channel_id=1, source_target_pairs={{0,1},{1,2},{2,3},{3,4},{4,5},{5,6},{6,7},{7,64},{64,65},{65,66},{... | collective-permute-start | bytes 12296 | tf_op jit(solution)/shard_map/ppermute | solution.py:27
  579.3 22.9 %collective-permute-start.80 = (f32[3,8,128]{2,1,0:T(8,128)S(1)}, f32[3,8,128]{2,1,0:T(8,128)S(1)}, u32[]{:S(2)}, u32[]{:S(2)}) collective-permute-start(f32[3,8,128]{2,1,0:T(8,128)S(1)} %get-tuple-element.95), channel_id=1, source_target_pairs={{0,1},{1,2},{2,3},{3,4},{4,5},{5,6},{6,7},{7,64},{64,65},{65,66},{... | collective-permute-start | bytes 36872 | tf_op jit(solution)/shard_map/ppermute | solution.py:27
  587.3 28.7 %collective-permute-start.68 = (f32[3,8,128]{2,1,0:T(8,128)}, f32[3,8,128]{2,1,0:T(8,128)S(1)}, u32[]{:S(2)}, u32[]{:S(2)}) collective-permute-start(f32[3,8,128]{2,1,0:T(8,128)} %get-tuple-element.88), channel_id=1, source_target_pairs={{0,1},{1,2},{2,3},{3,4},{4,5},{5,6},{6,7},{7,64},{64,65},{65,66},{... | collective-permute-start | bytes 36872 | tf_op jit(solution)/shard_map/ppermute | solution.py:27
  593.3 32.8 %collective-permute-start.73 = (f32[3,8,128]{2,1,0:T(8,128)}, f32[3,8,128]{2,1,0:T(8,128)S(1)}, u32[]{:S(2)}, u32[]{:S(2)}) collective-permute-start(f32[3,8,128]{2,1,0:T(8,128)} %get-tuple-element.94), channel_id=1, source_target_pairs={{1,0},{2,1},{3,2},{4,3},{5,4},{6,5},{7,6},{64,7},{65,64},{66,65},{... | collective-permute-start | bytes 36872 | tf_op jit(solution)/shard_map/ppermute | solution.py:29
  596.1 31.3 %collective-permute-start.72 = (f32[3,8,128]{2,1,0:T(8,128)}, f32[3,8,128]{2,1,0:T(8,128)S(1)}, u32[]{:S(2)}, u32[]{:S(2)}) collective-permute-start(f32[3,8,128]{2,1,0:T(8,128)} %get-tuple-element.93), channel_id=1, source_target_pairs={{0,1},{1,2},{2,3},{3,4},{4,5},{5,6},{6,7},{7,64},{64,65},{65,66},{... | collective-permute-start | bytes 36872 | tf_op jit(solution)/shard_map/ppermute | solution.py:27
  602.2 40.7 %collective-permute-start.67 = (f32[1,528,8]{2,1,0:T(8,128)}, f32[1,528,8]{2,1,0:T(8,128)}, u32[]{:S(2)}, u32[]{:S(2)}) collective-permute-start(f32[1,528,8]{2,1,0:T(8,128)} %get-tuple-element.169), channel_id=1, source_target_pairs={{8,0},{16,8},{24,16},{32,24},{40,32},{48,40},{56,48},{9,1},{17,9},... | collective-permute-start | bytes 50696 | tf_op jit(solution)/shard_map/ppermute | solution.py:29
  607.1 37.2 %collective-permute-start.66 = (f32[1,528,8]{2,1,0:T(8,128)}, f32[1,528,8]{2,1,0:T(8,128)}, u32[]{:S(2)}, u32[]{:S(2)}) collective-permute-start(f32[1,528,8]{2,1,0:T(8,128)} %get-tuple-element.168), channel_id=1, source_target_pairs={{0,8},{8,16},{16,24},{24,32},{32,40},{40,48},{48,56},{1,9},{9,17},... | collective-permute-start | bytes 50696 | tf_op jit(solution)/shard_map/ppermute | solution.py:27
  615.9 56.1 %collective-permute-start.83 = (f32[3,528,8]{1,2,0:T(8,128)}, f32[3,528,8]{1,2,0:T(8,128)}, u32[]{:S(2)}, u32[]{:S(2)}) collective-permute-start(f32[3,528,8]{1,2,0:T(8,128)} %copy.118), channel_id=1, source_target_pairs={{8,0},{16,8},{24,16},{32,24},{40,32},{48,40},{56,48},{9,1},{17,9},... | collective-permute-start | bytes 152072 | tf_op jit(solution)/shard_map/ppermute | solution.py:29
  626.1 26.1 %collective-permute-start.71 = (f32[3,528,8]{1,2,0:T(8,128)}, f32[3,528,8]{1,2,0:T(8,128)}, u32[]{:S(2)}, u32[]{:S(2)}) collective-permute-start(f32[3,528,8]{1,2,0:T(8,128)} %copy.110), channel_id=1, source_target_pairs={{8,0},{16,8},{24,16},{32,24},{40,32},{48,40},{56,48},{9,1},{17,9},... | collective-permute-start | bytes 152072 | tf_op jit(solution)/shard_map/ppermute | solution.py:29
  627.4 31.3 %collective-permute-start.70 = (f32[3,528,8]{1,2,0:T(8,128)}, f32[3,528,8]{1,2,0:T(8,128)}, u32[]{:S(2)}, u32[]{:S(2)}) collective-permute-start(f32[3,528,8]{1,2,0:T(8,128)} %copy.109), channel_id=1, source_target_pairs={{0,8},{8,16},{16,24},{24,32},{32,40},{40,48},{48,56},{1,9},{9,17},... | collective-permute-start | bytes 152072 | tf_op jit(solution)/shard_map/ppermute | solution.py:27
  (120 other events, 1196.3 us)
where the time goes:
time: 735 us; the launch traced here: 721 us
  starting transfers between devices  363 us (49%)
  other arithmetic  185 us (25%)
  local copies, waits for them, and re-layouts  159 us (22%)
  waiting for transfers between devices  10 us (1%)
    ppermute x42, starting transfers between devices, with_halo(): lax.ppermute(tail, axis, [(i, (i + 1) % count) for i in range(ends)])  254 us
    ppermute x42, starting transfers between devices, with_halo(): lax.ppermute(head, axis, [((i + 1) % count, i) for i in range(ends)])  69.2 us
    slice x49, local copies, waits for them, and re-layouts, with_halo(): lax.slice_in_dim(cells, cells.shape[dim] - width, cells.shape[dim], axis=...  52.3 us
    unnamed x8, other arithmetic  31.6 us
    add x16, other arithmetic, shards(): crop_cycle(source_deep, 1 + sweep) + SPREAD * neighbours(press_deep)  31 us
    slice x15, local copies, waits for them, and re-layouts, with_halo(): head = lax.slice_in_dim(cells, 0, width, axis=dim)  27.2 us
    ppermute x13, local copies, waits for them, and re-layouts, with_halo(): lax.ppermute(head, axis, [((i + 1) % count, i) for i in range(ends)])  26.9 us
    ppermute x13, local copies, waits for them, and re-layouts, with_halo(): lax.ppermute(tail, axis, [(i, (i + 1) % count) for i in range(ends)])  23.5 us
  transfers between devices with their start and end apart: 87, of which 2 were waited for; matrix products, arithmetic and copies ran while one was open for 37% of the time, Pallas kernels for 0%

commit v1 on v0

v1 whole, which is shorter than its diff:
```python
import functools

import jax
import jax.numpy as jnp
from jax import lax
from jax.experimental import pallas as pl
from jax.experimental.pallas import tpu as pltpu
from jax.sharding import PartitionSpec as P

LEVELS = 4
SWEEPS = 4
SPREAD = 0.25
GRAVITY_PUSH = 0.4
SOURCE = 2.0
SURFACE_STEP = 0.2
COURANT = 0.25
SLOPE_PULL = 0.5
LAYER_SHARE = (0.2, 0.3, 0.5)

LANES = 128
RIM = 32
PAD = 8
TOP = PAD + RIM
CHUNK = 32
WINDOW = (26, 19, 12, 5)
SHIFT = (26, 71, 102, 119)


def lane_of(shape):
    return lax.broadcasted_iota(jnp.int32, shape, len(shape) - 1)


def turn(value, shift):
    shift = shift % LANES
    return value if shift == 0 else pltpu.roll(value, shift, 1)


def east(value):
    return turn(value, -1) - turn(value, 1)


def edges_of(inner, lane):
    return jnp.where(lane < 64, turn(inner, 32), turn(inner, 96))


def slide_step(h, m, f, first, last):
    width = h.shape[1]

    def lo(v):
        return jnp.where(first, 0.0, pltpu.roll(v, 1, 1))

    def hi(v):
        return jnp.where(last, 0.0, pltpu.roll(v, width - 1, 1))

    u = m / (1.0 + jnp.abs(h))
    fm = m * u + 0.5 * h * h
    m_lo, m_hi = lo(m), hi(m)
    new_h = 0.5 * (lo(h) + hi(h)) - 0.5 * COURANT * (m_hi - m_lo)
    drag = f * h * u / jnp.sqrt(u * u + 1.0)
    new_m = (
        0.5 * (m_lo + m_hi)
        - 0.5 * COURANT * (hi(fm) - lo(fm))
        + COURANT * (SLOPE_PULL * h - drag)
    )
    return new_h, new_m


def kernel(
    dims,
    thick_in, foot_in, mom_in, fric_in, surf_in, fx_in, fy_in, bathy_in, table,
    surf_out, press_out, bottom_out, thick_out, mom_out,
    sl, foot, rise_s, pack_s, hm, hmt, rx, hh,
    eta, uu, vv, bathy, dep, pa, pb, ss, coef, mask, qq, rt, rpk, xs, xr, bq,
    load_sem, out_sem, ys_send, ys_recv, rise_send, rise_recv, rl_send, rl_recv,
    x_send, x_recv, hm_send, hm_recv, h2_send, h2_recv, b_send, b_recv, own_sem,
):
    nsec, ngx, ngy, tile_y, strip_w, cells_x, rc = dims
    bands = nsec * ngy
    rows = tile_y + 2 * RIM
    s, g, y = lax.axis_index("sec"), lax.axis_index("gx"), lax.axis_index("gy")
    b = s * ngy + y

    def along_gx(j):
        return (s, lax.rem(g + j + ngx, ngx), y)

    def along_band(j):
        other = lax.rem(b + j + bands, bands)
        return (other // ngy, g, lax.rem(other, ngy))

    def remote(src, dst, send, recv, device):
        return pltpu.make_async_remote_copy(
            src_ref=src, dst_ref=dst, send_sem=send, recv_sem=recv,
            device_id=device, device_id_type=pl.DeviceIdType.MESH,
        )

    own_rows = pl.ds(TOP, tile_y)
    loads = [
        pltpu.make_async_copy(thick_in.at[0, 0], sl.at[0], load_sem.at[0]),
        pltpu.make_async_copy(foot_in.at[0, 0], foot, load_sem.at[1]),
        pltpu.make_async_copy(mom_in.at[0, 0], sl.at[1], load_sem.at[2]),
        pltpu.make_async_copy(fric_in.at[0, 0], sl.at[2], load_sem.at[3]),
        pltpu.make_async_copy(surf_in, eta.at[0, own_rows], load_sem.at[4]),
        pltpu.make_async_copy(fx_in, uu.at[0, :, own_rows], load_sem.at[5]),
        pltpu.make_async_copy(fy_in, vv.at[0, :, own_rows], load_sem.at[6]),
        pltpu.make_async_copy(bathy_in, bathy.at[own_rows], load_sem.at[7]),
    ]
    for copy in loads:
        copy.start()

    barrier = pltpu.get_barrier_semaphore()
    partners = [along_gx(j) for j in range(1, ngx)] + [along_band(j) for j in range(1, bands)]
    for device in partners:
        pl.semaphore_signal(barrier, inc=1, device_id=device, device_id_type=pl.DeviceIdType.MESH)
    pl.semaphore_wait(barrier, len(partners))

    low, high = pl.ds(PAD, RIM), pl.ds(TOP + tile_y, RIM)
    first_rows, last_rows = pl.ds(0, RIM), pl.ds(tile_y - RIM, RIM)
    y_copies = []
    for n, (src, dst) in enumerate(
        (
            (lambda r: surf_in.at[r], lambda r: eta.at[0, r]),
            (lambda r: fx_in.at[:, r], lambda r: uu.at[0, :, r]),
            (lambda r: fy_in.at[:, r], lambda r: vv.at[0, :, r]),
            (lambda r: bathy_in.at[r], lambda r: bathy.at[r]),
        )
    ):
        y_copies.append(
            remote(src(first_rows), dst(high), ys_send.at[0, n], ys_recv.at[0, n], along_band(-1))
        )
        y_copies.append(
            remote(src(last_rows), dst(low), ys_send.at[1, n], ys_recv.at[1, n], along_band(1))
        )
    for copy in y_copies:
        copy.start()

    for copy in loads[:4]:
        copy.wait()

    def slide_rows(i, carry):
        r = pl.ds(pl.multiple_of(i * 8, 8), 8)
        lane = lane_of((8, cells_x))
        first, last = lane == 0, lane == cells_x - 1
        h = sl[0, r] * foot[r].astype(jnp.float32)
        m, f = sl[1, r], sl[2, r]
        for level in range(LEVELS):
            new_h, m = slide_step(h, m, f, first, last)
            rise = new_h - h
            for j in range(ngx):
                rise_s[level, j, r] = rise[:, j * LANES : (j + 1) * LANES]
            h = new_h
        hm[r] = h
        hm[pl.ds(pl.multiple_of(i * 8 + strip_w, 8), 8)] = m
        return carry

    lax.fori_loop(0, strip_w // 8, slide_rows, 0)

    def strip_rows(j):
        return pl.ds(pl.multiple_of(TOP + j * strip_w, 8), strip_w)

    def rise_copies(n, src, dst):
        copies = []
        for j in range(1, ngx):
            device = along_gx(j)
            copies.append(
                remote(
                    src(device[1]), dst(strip_rows(g)),
                    rise_send.at[n, j], rise_recv.at[n, j], device,
                )
            )
        own = pltpu.make_async_copy(src(g), dst(strip_rows(g)), own_sem.at[n])
        return copies + [own]

    rises = [
        rise_copies(n, lambda j, n=n: rise_s.at[n, j], lambda r, n=n: rt.at[0, n, r])
        for n in range(LEVELS)
    ]
    rises.append(rise_copies(LEVELS, lambda j: pack_s.at[j], lambda r: rpk.at[r]))

    def start(copies):
        for copy in copies:
            copy.start()

    def finish_recv(copies):
        for copy in copies[:-1]:
            copy.wait_recv()
        copies[-1].wait()

    start(rises[0])

    def relays(n, ref):
        return [
            remote(
                ref(pl.ds(TOP, RIM)), ref(high), rl_send.at[0, n], rl_recv.at[0, n], along_band(-1)
            ),
            remote(
                ref(pl.ds(TOP + tile_y - RIM, RIM)), ref(low),
                rl_send.at[1, n], rl_recv.at[1, n], along_band(1),
            ),
        ]

    relay = [relays(n, lambda r, n=n: rt.at[0, n, r]) for n in range(LEVELS)]
    relay.append(relays(LEVELS, lambda r: rpk.at[r]))

    def over_rows(fn, lo=PAD, hi=PAD + rows, step=CHUNK):
        def body(i, carry):
            fn(pl.multiple_of(lo + i * step, 8))
            return carry

        lax.fori_loop(0, (hi - lo) // step, body, 0)

    zero = jnp.zeros((RIM, LANES), jnp.float32)

    def clear_outside(refs):
        @pl.when(b == 0)
        def _():
            for ref in refs:
                ref(low)[...] = zero

        @pl.when(b == bands - 1)
        def _():
            for ref in refs:
                ref(high)[...] = zero

    for copy in loads[4:]:
        copy.wait()
    for copy in y_copies:
        copy.wait_recv()
    clear_outside(
        [lambda r: eta.at[0, r]]
        + [lambda r, k=k: uu.at[0, k, r] for k in range(3)]
        + [lambda r, k=k: vv.at[0, k, r] for k in range(3)]
    )

    def prepare(r):
        here = pl.ds(r, CHUNK)
        lane = lane_of((CHUNK, LANES))
        kind = bathy[here]
        depth = jnp.zeros((CHUNK, LANES), jnp.float32)
        for c in range(table.shape[0]):
            depth = jnp.where(kind == c, table[c], depth)
        dep[0, here] = depth
        dep[1, here] = edges_of(depth, lane)
        eta[1, here] = edges_of(eta[0, here], lane)
        for k in range(3):
            uu[1, k, here] = edges_of(uu[0, k, here], lane)
            vv[1, k, here] = edges_of(vv[0, k, here], lane)
        fields = (
            (eta[0, here], uu[0, 0, here], uu[0, 1, here], uu[0, 2, here]),
            (vv[0, 0, here], vv[0, 1, here], vv[0, 2, here], depth),
        )
        for unit, four in enumerate(fields):
            right = turn(four[0], 32)
            left = four[0]
            for q in range(1, 4):
                right = jnp.where(lane >= 32 * q, turn(four[q], 32 * q + 32), right)
                left = jnp.where(lane >= 32 * q, turn(four[q], 32 * q), left)
            xs[0, unit, here] = right
            xs[1, unit, here] = left
        row = r + lax.broadcasted_iota(jnp.int32, (CHUNK, LANES), 0)
        inside = ((row >= TOP) | (b > 0)) & ((row < TOP + tile_y) | (b < bands - 1))
        inside_columns = ((lane >= 32) | (g > 0)) & ((lane < 96) | (g < ngx - 1))
        mask[0, here] = inside.astype(jnp.float32)
        mask[1, here] = (inside & inside_columns).astype(jnp.float32)

    over_rows(prepare)

    every = pl.ds(PAD, rows)
    x_copies = []
    for unit in range(2):
        x_copies.append(
            remote(
                xs.at[0, unit, every], xr.at[0, unit, every],
                x_send.at[0, unit], x_recv.at[0, unit], along_gx(1),
            )
        )
        x_copies.append(
            remote(
                xs.at[1, unit, every], xr.at[1, unit, every],
                x_send.at[1, unit], x_recv.at[1, unit], along_gx(-1),
            )
        )
    start(x_copies)
    start(rises[1])

    def pack_rows(i, carry):
        r = pl.ds(pl.multiple_of(i * 8, 8), 8)
        lane = lane_of((8, LANES))
        for j in range(ngx):
            packed = None
            at = 0
            for level in range(LEVELS):
                ring = jnp.where(
                    lane < 64,
                    rise_s[level, min(j + 1, ngx - 1), r],
                    rise_s[level, max(j - 1, 0), r],
                )
                ring = turn(ring, SHIFT[level])
                packed = ring if packed is None else jnp.where(lane >= at, ring, packed)
                at += 2 * WINDOW[level]
            pack_s[j, r] = packed
        return carry

    lax.fori_loop(0, strip_w // 8, pack_rows, 0)
    start(rises[4])
    start(rises[2])
    start(rises[3])

    block = ngy * rc
    for j in range(cells_x // LANES):
        turned = hm[:, j * LANES : (j + 1) * LANES].T
        for part in range(LANES // min(block, LANES)):
            size = min(block, LANES)
            x0 = j * LANES + part * size
            group = x0 // block
            hmt[group // ngx, group % ngx, pl.ds(x0 % block, size)] = turned[
                part * size : (part + 1) * size
            ]
    hm_copies = []
    for j in range(1, ngx):
        device = along_gx(j)
        hm_copies.append(
            remote(hmt.at[:, device[1]], rx.at[g], hm_send.at[j], hm_recv.at[j], device)
        )
    hm_copies.append(pltpu.make_async_copy(hmt.at[:, g], rx.at[g], own_sem.at[5]))
    start(hm_copies)

    def invert(p):
        def rows_of(r):
            here = pl.ds(r, CHUNK)
            depth = dep[p, here]
            scale = mask[p, here] * SPREAD
            k = 9.0 / (depth * depth)
            i1 = 1.0 / (1.0 + 3.0 * k)
            l1 = k * i1
            i2 = 1.0 / (1.0 + 2.0 * k - k * l1)
            l2 = k * i2
            i3 = 1.0 / (1.0 + k - k * l2)
            coef[p, 0, here] = l1
            coef[p, 1, here] = l2
            coef[p, 2, here] = i1 * scale
            coef[p, 3, here] = i2 * scale
            coef[p, 4, here] = i3 * scale

        over_rows(rows_of)

    def solve(p, here, v):
        l1, l2 = coef[p, 0, here], coef[p, 1, here]
        y2 = v[1] + l1 * v[0]
        y3 = v[2] + l2 * y2
        x3 = y3 * coef[p, 4, here]
        x2 = y2 * coef[p, 3, here] + l2 * x3
        x1 = v[0] * coef[p, 2, here] + l1 * x2
        return x1, x2, x3

    def predict(p):
        def rows_of(r):
            here, up, down = pl.ds(r, CHUNK), pl.ds(r + 1, CHUNK), pl.ds(r - 1, CHUNK)
            push = mask[p, here] * (0.5 * GRAVITY_PUSH)
            ge = push * east(eta[p, here])
            gn = push * (eta[p, up] - eta[p, down])
            for k in range(3):
                uu[p, k, here] = uu[p, k, here] - ge
                vv[p, k, here] = vv[p, k, here] - gn

        over_rows(rows_of)

    def source(p, level):
        def rows_of(r):
            here, up, down = pl.ds(r, CHUNK), pl.ds(r + 1, CHUNK), pl.ds(r - 1, CHUNK)
            rise = rt[p, level, here]
            v = []
            for k in range(3):
                spread = east(uu[p, k, here]) + (vv[p, k, up] - vv[p, k, down])
                v.append((4.0 * SOURCE * LAYER_SHARE[k]) * rise - 2.0 * spread)
                ss[p, k, here] = v[k]
            if level == 0:
                for k, value in enumerate(solve(p, here, v)):
                    pb[p, k, here] = value

        over_rows(rows_of)

    def sweep(p, old, new):
        def rows_of(r):
            here, up, down = pl.ds(r, CHUNK), pl.ds(r + 1, CHUNK), pl.ds(r - 1, CHUNK)
            v = []
            for k in range(3):
                c = old[p, k, here]
                v.append(
                    (ss[p, k, here] + (turn(c, -1) + turn(c, 1)))
                    + (old[p, k, up] + old[p, k, down])
                )
            for k, value in enumerate(solve(p, here, v)):
                new[p, k, here] = value

        over_rows(rows_of)

    def correct(p, level):
        def rows_of(r):
            here, up, down = pl.ds(r, CHUNK), pl.ds(r + 1, CHUNK), pl.ds(r - 1, CHUNK)
            push = mask[p, here] * (0.5 * SPREAD)
            for k in range(3):
                c = pa[p, k, here]
                uu[p, k, here] = uu[p, k, here] - push * east(c)
                vv[p, k, here] = vv[p, k, here] - push * (pa[p, k, up] - pa[p, k, down])
            c = c * (1.0 / LEVELS)
            qq[p, here] = c if level == 0 else qq[p, here] + c

        over_rows(rows_of)

    def raise_surface(p, level):
        def rows_of(r):
            here, up, down = pl.ds(r, CHUNK), pl.ds(r + 1, CHUNK), pl.ds(r - 1, CHUNK)
            push = mask[p, here] * (0.5 * SURFACE_STEP)
            total = uu[p, 0, here] + uu[p, 1, here] + uu[p, 2, here]
            north = (vv[p, 0, up] + vv[p, 1, up] + vv[p, 2, up]) - (
                vv[p, 0, down] + vv[p, 1, down] + vv[p, 2, down]
            )
            eta[p, here] = eta[p, here] - push * (east(total) + north) + rt[p, level, here]

        over_rows(rows_of)

    def sweeps(p, level):
        if level > 0:
            sweep(p, pa, pb)
        sweep(p, pb, pa)
        sweep(p, pa, pb)
        sweep(p, pb, pa)

    def start_relay(n):
        finish_recv(rises[n])
        start(relay[n])

    def end_relay(n):
        for copy in relay[n]:
            copy.wait_recv()
        if n < LEVELS:
            clear_outside([lambda r: rt.at[0, n, r]])

    def level_of(p, level, between=()):
        predict(p)
        if between:
            between[0]()
        source(p, level)
        if len(between) > 1:
            between[1]()
        sweeps(p, level)
        correct(p, level)
        raise_surface(p, level)

    start_relay(0)
    invert(0)
    level_of(0, 0, (lambda: end_relay(0), lambda: start_relay(1)))

    finish_recv(hm_copies)
    lane64 = lane_of((block, LANES)) < 64
    for part in range(nsec):
        for p in range(ngx // 2):
            one, two = rx[2 * p, part], rx[2 * p + 1, part]
            columns = pl.ds(p * LANES, LANES)
            hh[0, part, :, columns] = jnp.where(lane64, one, turn(two, 64))
            hh[1, part, :, columns] = jnp.where(lane64, turn(one, 64), two)
    band_columns = pl.ds(pl.multiple_of(b * tile_y, LANES), tile_y)
    h2_copies = []
    for which, out in enumerate((thick_out, mom_out)):
        for j in range(1, bands):
            device = along_band(j)
            h2_copies.append(
                remote(
                    hh.at[which, device[0], pl.ds(pl.multiple_of(device[2] * rc, 8), rc)],
                    out.at[:, band_columns],
                    h2_send.at[which, j], h2_recv.at[which, j], device,
                )
            )
    for which, out in enumerate((thick_out, mom_out)):
        h2_copies.append(
            pltpu.make_async_copy(
                hh.at[which, s, pl.ds(pl.multiple_of(y * rc, 8), rc)],
                out.at[:, band_columns],
                own_sem.at[6 + which],
            )
        )
    start(h2_copies)

    level_of(0, 1, (lambda: end_relay(1), lambda: None))

    for n in (4, 2, 3):
        start_relay(n)
    for copy in x_copies:
        copy.wait_recv()
    for n in (4, 2, 3):
        end_relay(n)

    def edge_rows(r):
        here = pl.ds(r, CHUNK)
        lane = lane_of((CHUNK, LANES))
        inside = mask[1, here] > 0.0

        def put(left, inner, right, fill=0.0):
            value = jnp.where(lane < 32, left, jnp.where(lane < 96, inner, right))
            return jnp.where(inside, value, fill)

        left, right = xr[0, 0, here], xr[1, 0, here]
        eta[1, here] = put(left, eta[1, here], turn(right, 96))
        for k in range(3):
            q = k + 1
            uu[1, k, here] = put(turn(left, -32 * q), uu[1, k, here], turn(right, 96 - 32 * q))
        left, right = xr[0, 1, here], xr[1, 1, here]
        for k in range(3):
            vv[1, k, here] = put(turn(left, -32 * k), vv[1, k, here], turn(right, 96 - 32 * k))
        dep[1, here] = put(turn(left, -96), dep[1, here], right, 1.0)
        packed = rpk[here]
        for level in range(LEVELS):
            rt[1, level, here] = put(
                turn(packed, 32 - SHIFT[level]),
                edges_of(rt[0, level, here], lane),
                turn(packed, 96 - SHIFT[level]),
            )

    over_rows(edge_rows)
    invert(1)
    level_of(1, 0)
    level_of(1, 1)

    def merged(inner, edge, lane):
        return jnp.where(
            lane < 16, turn(edge, 96), jnp.where(lane >= 112, turn(edge, 32), inner)
        )

    def merge_rows(r):
        here = pl.ds(r, CHUNK)
        lane = lane_of((CHUNK, LANES))
        refs = [lambda p: eta.at[p]]
        for k in range(3):
            refs += [
                lambda p, k=k: uu.at[p, k], lambda p, k=k: vv.at[p, k], lambda p, k=k: pa.at[p, k]
            ]
        for ref in refs:
            inner, edge = ref(0)[here], ref(1)[here]
            ref(0)[here] = merged(inner, edge, lane)
            ref(1)[here] = jnp.where(
                (lane >= 48) & (lane < 80), edges_of(inner, lane), edge
            )

    over_rows(merge_rows)
    for level in range(2, LEVELS):
        for p in range(2):
            level_of(p, level)

    def last_rows_of(r):
        here = pl.ds(r, CHUNK)
        lane = lane_of((CHUNK, LANES))
        bq[pl.ds(pl.multiple_of(r - TOP, 8), CHUNK)] = merged(qq[0, here], qq[1, here], lane)
        eta[0, here] = merged(eta[0, here], eta[1, here], lane)
        for k in range(3):
            pa[0, k, here] = merged(pa[0, k, here], pa[1, k, here], lane)

    over_rows(last_rows_of, TOP, TOP + tile_y)

    b_copies = []
    columns = pl.ds(pl.multiple_of(g * LANES, LANES), LANES)

    def of_strip(j):
        return bq.at[pl.ds(pl.multiple_of(j * strip_w, 8), strip_w)]

    for j in range(1, ngx):
        device = along_gx(j)
        b_copies.append(
            remote(
                of_strip(device[1]), bottom_out.at[0, 0, :, columns],
                b_send.at[j], b_recv.at[j], device,
            )
        )
    b_copies.append(
        pltpu.make_async_copy(of_strip(g), bottom_out.at[0, 0, :, columns], own_sem.at[8])
    )
    start(b_copies)
    outs = [
        pltpu.make_async_copy(eta.at[0, own_rows], surf_out, out_sem.at[0]),
        pltpu.make_async_copy(pa.at[0, :, own_rows], press_out, out_sem.at[1]),
    ]
    start(outs)
    finish_recv(b_copies)
    for copy in h2_copies[:-2]:
        copy.wait_recv()
    for copy in h2_copies[-2:] + outs:
        copy.wait()
    for copies in rises + [hm_copies, b_copies]:
        for copy in copies[:-1]:
            copy.wait_send()
    for copies in relay + [y_copies, x_copies, h2_copies[:-2]]:
        for copy in copies:
            copy.wait_send()


def shards(
    slide_thickness, footprint, slide_momentum, bed_friction, surface, flux_x, flux_y,
    bathy_class, depth_table,
):
    nsec, ngx, ngy = (lax.axis_size(a) for a in ("sec", "gx", "gy"))
    _, _, strip_w, cells_x = slide_thickness.shape
    tile_y, tile_x = surface.shape
    assert tile_x == LANES and strip_w * 2 == LANES and strip_w * ngx == tile_y
    rc = cells_x // (nsec * ngx * ngy)
    bands = nsec * ngy
    array_rows = tile_y + 2 * TOP
    f32 = jnp.float32
    plane = (2, array_rows, LANES)
    three = (2, 3, array_rows, LANES)
    dma = pltpu.SemaphoreType.DMA
    anywhere = pl.BlockSpec(memory_space=pl.ANY)
    return pl.pallas_call(
        functools.partial(kernel, (nsec, ngx, ngy, tile_y, strip_w, cells_x, rc)),
        out_shape=(
            jax.ShapeDtypeStruct(surface.shape, f32),
            jax.ShapeDtypeStruct(flux_x.shape, f32),
            jax.ShapeDtypeStruct(slide_thickness.shape, f32),
            jax.ShapeDtypeStruct((rc, tile_y * bands), f32),
            jax.ShapeDtypeStruct((rc, tile_y * bands), f32),
        ),
        in_specs=[anywhere] * 8 + [pl.BlockSpec(memory_space=pltpu.SMEM)],
        out_specs=(anywhere,) * 5,
        scratch_shapes=[
            pltpu.VMEM((3, strip_w, cells_x), f32),
            pltpu.VMEM((strip_w, cells_x), jnp.int32),
            pltpu.VMEM((LEVELS, ngx, strip_w, LANES), f32),
            pltpu.VMEM((ngx, strip_w, LANES), f32),
            pltpu.VMEM((2 * strip_w, cells_x), f32),
            pltpu.VMEM((nsec, ngx, ngy * rc, LANES), f32),
            pltpu.VMEM((ngx, nsec, ngy * rc, LANES), f32),
            pltpu.VMEM((2, nsec, ngy * rc, tile_y), f32),
            pltpu.VMEM(plane, f32),
            pltpu.VMEM(three, f32),
            pltpu.VMEM(three, f32),
            pltpu.VMEM((array_rows, LANES), jnp.int32),
            pltpu.VMEM(plane, f32),
            pltpu.VMEM(three, f32),
            pltpu.VMEM(three, f32),
            pltpu.VMEM(three, f32),
            pltpu.VMEM((2, 5, array_rows, LANES), f32),
            pltpu.VMEM(plane, f32),
            pltpu.VMEM(plane, f32),
            pltpu.VMEM((2, LEVELS, array_rows, LANES), f32),
            pltpu.VMEM((array_rows, LANES), f32),
            pltpu.VMEM((2, 2, array_rows, LANES), f32),
            pltpu.VMEM((2, 2, array_rows, LANES), f32),
            pltpu.VMEM((tile_y, LANES), f32),
            dma((8,)),
            dma((2,)),
            dma((2, 4)), dma((2, 4)),
            dma((LEVELS + 1, ngx)), dma((LEVELS + 1, ngx)),
            dma((2, LEVELS + 1)), dma((2, LEVELS + 1)),
            dma((2, 2)), dma((2, 2)),
            dma((ngx,)), dma((ngx,)),
            dma((2, bands)), dma((2, bands)),
            dma((ngx,)), dma((ngx,)),
            dma((9,)),
        ],
        compiler_params=pltpu.CompilerParams(
            collective_id=0, has_side_effects=True, vmem_limit_bytes=56 * 2**20
        ),
    )(
        slide_thickness, footprint, slide_momentum, bed_friction, surface, flux_x, flux_y,
        bathy_class, depth_table,
    )


def solution(mesh):
    strips = P(("sec", "gy"), "gx", None, None)
    tiles = P(("sec", "gy"), "gx")
    layers = P(None, ("sec", "gy"), "gx")
    turned = P(("sec", "gx", "gy"), None)
    return jax.shard_map(
        shards,
        mesh=mesh,
        in_specs=(strips,) * 4 + (tiles, layers, layers, tiles, P()),
        out_specs=(tiles, layers, strips, turned, turned),
        check_vma=False,
    )
```

time: 735 us -> 190 us (0.26); the launches traced: 721 us -> 189 us
  starting transfers between devices: 363 us -> 0 us
  other arithmetic: 185 us -> 0 us
  Pallas kernels: 0 us -> 181 us
  local copies, waits for them, and re-layouts: 159 us -> 6.57 us
  waiting for transfers between devices: 10 us -> 0 us
    ppermute x84 -> x0, starting transfers between devices: 323 us -> none  [the longest x42 254 us: with_halo(): lax.ppermute(tail, axis, [(i, (i + 1) % count) for i in range(ends)])]
    pallas_call x0 -> x1, Pallas kernels: none -> 181 us  [shards(): pl.pallas_call(functools.partial(kernel, (nsec, ngx, ngy, tile_y, strip_w...]
    slice x76 -> x0, local copies, waits for them, and re-layouts: 88 us -> none  [the longest x49 52.3 us: with_halo(): lax.slice_in_dim(cells, cells.shape[dim] - width, cells.shape[dim], axis=...]
    add x41 -> x0, other arithmetic: 59.3 us -> none  [the longest x16 31 us: shards(): crop_cycle(source_deep, 1 + sweep) + SPREAD * neighbours(press_deep)]
    ppermute x26 -> x0, local copies, waits for them, and re-layouts: 50.3 us -> none  [the longest x13 26.9 us: with_halo(): lax.ppermute(head, axis, [((i + 1) % count, i) for i in range(ends)])]
    all_to_all x3 -> x0, starting transfers between devices: 40.2 us -> none  [the longest x1 16.1 us: shards(): lax.all_to_all(stacked, 'gx', split_axis=2, concat_axis=1, tiled=True)]
    mul x12 -> x0, other arithmetic: 36.3 us -> none  [the longest x4 19.8 us: shards(): (crop_cycle(wide_east, 1) - GRAVITY_PUSH * diff_east(eta_wide)) * crop_cy...]
    unnamed x8 -> x0, other arithmetic: 31.6 us -> none
  transfers between devices with their start and end apart: 87 -> 0, of which waited for: 2 -> 0; matrix products, arithmetic and copies ran while one was open for 37% -> 0% of each run, Pallas kernels for 0% -> 0%
where the time goes in v1:
time: 190 us; the launch traced here: 189 us
  Pallas kernels  181 us (95%)
  local copies, waits for them, and re-layouts  6.57 us (3%)
    pallas_call x1, Pallas kernels, shards(): pl.pallas_call(functools.partial(kernel, (nsec, ngx, ngy, tile_y, strip_w...  181 us
    unnamed x11, local copies, waits for them, and re-layouts  6.57 us

profile of v1, /device:TPU:24, one launch (start us, length us, event | category | flops | bytes accessed | tf_op | source)
XLA Modules:
  0.0 188.6 jit_solution(12057757699015399661)
XLA Ops:
  0.6 181.4 %shard_map.128 = (f32[512,128]{1,0:T(8,128)}, f32[3,512,128]{2,1,0:T(8,128)}, f32[1,1,64,1024]{3,2,1,0:T(8,128)}, f32[8,8192]{1,0:T(8,128)}, f32[8,8192]{1,0:T(8,128)}) custom-call(f32[1,1,64,1024]{3,2,1,0:T(8,128)} %thick_in.1, s32[1,1,64,1024]{3,2,1,0:T(8,128)} %foot_in.1, f32[1,1,64,1024]{3,2,1,0:T(8,128)} %mom_in.1, f32[1,1,64,1024]{3,2,1,0:T(8,128)} %fric_in.1, ...), custom_call_target="tpu_custom_call" | custom-call | tf_op jit(solution)/shard_map/pallas_call | solution.py:611
  182.0 1.7 copy.19
  183.7 0.0 copy-start.2
  183.7 2.1 %copy.20 = f32[3,512,128]{2,1,0:T(8,128)} copy(f32[3,512,128]{2,1,0:T(8,128)} %get-tuple-element.11) | data formatting | bytes 1572864
  185.8 0.0 copy-done.2
  185.8 0.0 copy-start.1
  185.8 0.7 copy.21
  186.5 0.3 copy-done.1
  186.8 0.0 copy-start
  186.8 0.7 copy.22
  187.5 0.3 copy-done
  187.9 0.7 copy.23
Async XLA Ops:
  183.7 2.1 %copy-start.2 = (f32[1,1,64,1024]{3,2,1,0:T(8,128)S(1)}, f32[1,1,64,1024]{3,2,1,0:T(8,128)}, u32[]{:S(2)}) copy-start(f32[1,1,64,1024]{3,2,1,0:T(8,128)} %get-tuple-element.12) | copy-start | bytes 786436
  185.8 1.0 copy-start.1
  186.8 1.0 copy-start

commit v2 on v1

v2 whole, which is shorter than its diff:
```python
import functools

import jax
import jax.numpy as jnp
from jax import lax
from jax.experimental import pallas as pl
from jax.experimental.pallas import tpu as pltpu
from jax.sharding import PartitionSpec as P

LEVELS = 4
SWEEPS = 4
SPREAD = 0.25
GRAVITY_PUSH = 0.4
SOURCE = 2.0
SURFACE_STEP = 0.2
COURANT = 0.25
SLOPE_PULL = 0.5
LAYER_SHARE = (0.2, 0.3, 0.5)

LANES = 128
JS = 5
RIM = 32
UNROLL = 4
PAD = 8
TOP = PAD + RIM
WINDOW = (26, 19, 12, 5)
SHIFT = (26, 71, 102, 119)


def lane_of(shape):
    return lax.broadcasted_iota(jnp.int32, shape, len(shape) - 1)


def turn(value, shift):
    shift = shift % LANES
    return value if shift == 0 else pltpu.roll(value, shift, 1)


def slide_step(h, m, f, first, last):
    width = h.shape[1]

    def lo(v):
        return jnp.where(first, 0.0, pltpu.roll(v, 1, 1))

    def hi(v):
        return jnp.where(last, 0.0, pltpu.roll(v, width - 1, 1))

    u = m / (1.0 + jnp.abs(h))
    fm = m * u + 0.5 * h * h
    m_lo, m_hi = lo(m), hi(m)
    new_h = 0.5 * (lo(h) + hi(h)) - 0.5 * COURANT * (m_hi - m_lo)
    drag = f * h * u / jnp.sqrt(u * u + 1.0)
    new_m = (
        0.5 * (m_lo + m_hi)
        - 0.5 * COURANT * (hi(fm) - lo(fm))
        + COURANT * (SLOPE_PULL * h - drag)
    )
    return new_h, new_m


def kernel(
    dims,
    thick_in, foot_in, mom_in, fric_in, surf_in, fx_in, fy_in, bathy_in, table,
    surf_out, press_out, bottom_out, thick_out, mom_out,
    sl, foot, rise_s, pack_s, hm, hmt, rx, hh,
    wide, kinds, wide_rise,
    eta, uu, vv, dep, pa, pb, ss, coef, mask, qq, rt, back,
    load_sem, out_sem, ys_send, ys_recv, rise_send, rise_recv, rl_send, rl_recv,
    x_send, x_recv, hm_send, hm_recv, h2_send, h2_recv, b_send, b_recv, own_sem,
):
    nsec, ngx, ngy, tile_y, strip_w, cells_x, rc = dims
    bands = nsec * ngy
    tile_x = LANES
    s, g, y = lax.axis_index("sec"), lax.axis_index("gx"), lax.axis_index("gy")
    b = s * ngy + y

    def along_gx(j):
        return (s, lax.rem(g + j + ngx, ngx), y)

    def along_band(j):
        other = lax.rem(b + j + bands, bands)
        return (other // ngy, g, lax.rem(other, ngy))

    def remote(src, dst, send, recv, device):
        return pltpu.make_async_remote_copy(
            src_ref=src, dst_ref=dst, send_sem=send, recv_sem=recv,
            device_id=device, device_id_type=pl.DeviceIdType.MESH,
        )

    def start(copies):
        for copy in copies:
            copy.start()

    def finish_recv(copies):
        for copy in copies[:-1]:
            copy.wait_recv()
        copies[-1].wait()

    own_rows = pl.ds(RIM, tile_y)
    loads = [
        pltpu.make_async_copy(thick_in.at[0, 0], sl.at[0], load_sem.at[0]),
        pltpu.make_async_copy(foot_in.at[0, 0], foot, load_sem.at[1]),
        pltpu.make_async_copy(mom_in.at[0, 0], sl.at[1], load_sem.at[2]),
        pltpu.make_async_copy(fric_in.at[0, 0], sl.at[2], load_sem.at[3]),
        pltpu.make_async_copy(surf_in, wide.at[0, own_rows], load_sem.at[4]),
        pltpu.make_async_copy(fx_in, wide.at[pl.ds(1, 3), own_rows], load_sem.at[5]),
        pltpu.make_async_copy(fy_in, wide.at[pl.ds(4, 3), own_rows], load_sem.at[6]),
        pltpu.make_async_copy(bathy_in, kinds.at[own_rows], load_sem.at[7]),
    ]
    start(loads)

    barrier = pltpu.get_barrier_semaphore()
    partners = [along_gx(j) for j in range(1, ngx)] + [along_band(j) for j in range(1, bands)]
    for device in partners:
        pl.semaphore_signal(barrier, inc=1, device_id=device, device_id_type=pl.DeviceIdType.MESH)

    for copy in loads[:4]:
        copy.wait()

    def slide_rows(i, carry):
        r = pl.ds(pl.multiple_of(i * 8, 8), 8)
        lane = lane_of((8, cells_x))
        first, last = lane == 0, lane == cells_x - 1
        h = sl[0, r] * foot[r].astype(jnp.float32)
        m, f = sl[1, r], sl[2, r]
        for level in range(LEVELS):
            new_h, m = slide_step(h, m, f, first, last)
            rise = new_h - h
            for j in range(ngx):
                rise_s[level, j, r] = rise[:, j * LANES : (j + 1) * LANES]
            h = new_h
        hm[r] = h
        hm[pl.ds(pl.multiple_of(i * 8 + strip_w, 8), 8)] = m
        return carry

    lax.fori_loop(0, strip_w // 8, slide_rows, 0)

    def pack_rows(i, carry):
        r = pl.ds(pl.multiple_of(i * 16, 16), 16)
        lane = lane_of((16, LANES))
        for j in range(ngx):
            packed = None
            at = 0
            for level in range(LEVELS):
                ring = jnp.where(
                    lane < 64,
                    rise_s[level, min(j + 1, ngx - 1), r],
                    rise_s[level, max(j - 1, 0), r],
                )
                ring = turn(ring, SHIFT[level])
                packed = ring if packed is None else jnp.where(lane >= at, ring, packed)
                at += 2 * WINDOW[level]
            pack_s[j, r] = packed
        return carry

    lax.fori_loop(0, strip_w // 16, pack_rows, 0)

    pl.semaphore_wait(barrier, len(partners))

    low, high = pl.ds(0, RIM), pl.ds(RIM + tile_y, RIM)
    first_rows, last_rows = pl.ds(0, RIM), pl.ds(tile_y - RIM, RIM)
    y_copies = []
    for n, (src, dst) in enumerate(
        (
            (lambda r: surf_in.at[r], lambda r: wide.at[0, r]),
            (lambda r: fx_in.at[:, r], lambda r: wide.at[pl.ds(1, 3), r]),
            (lambda r: fy_in.at[:, r], lambda r: wide.at[pl.ds(4, 3), r]),
            (lambda r: bathy_in.at[r], lambda r: kinds.at[r]),
        )
    ):
        y_copies.append(
            remote(src(first_rows), dst(high), ys_send.at[0, n], ys_recv.at[0, n], along_band(-1))
        )
        y_copies.append(
            remote(src(last_rows), dst(low), ys_send.at[1, n], ys_recv.at[1, n], along_band(1))
        )
    start(y_copies)

    def strip_rows(j):
        return pl.ds(pl.multiple_of(RIM + j * strip_w, 8), strip_w)

    def rise_copies(n, src):
        copies = []
        for j in range(1, ngx):
            device = along_gx(j)
            copies.append(
                remote(
                    src(device[1]), wide_rise.at[n, strip_rows(g)],
                    rise_send.at[n, j], rise_recv.at[n, j], device,
                )
            )
        own = pltpu.make_async_copy(src(g), wide_rise.at[n, strip_rows(g)], own_sem.at[n])
        return copies + [own]

    rises = [rise_copies(n, lambda j, n=n: rise_s.at[n, j]) for n in range(LEVELS)]
    rises.append(rise_copies(LEVELS, lambda j: pack_s.at[j]))
    relay = []
    for n in range(LEVELS + 1):
        ref = wide_rise.at[n]
        relay.append(
            [
                remote(
                    ref.at[pl.ds(RIM, RIM)], ref.at[high],
                    rl_send.at[0, n], rl_recv.at[0, n], along_band(-1),
                ),
                remote(
                    ref.at[pl.ds(tile_y, RIM)], ref.at[low],
                    rl_send.at[1, n], rl_recv.at[1, n], along_band(1),
                ),
            ]
        )
    order = (0, 4, 1, 2, 3)
    for n in order[:2]:
        start(rises[n])

    zero = jnp.zeros((RIM, LANES), jnp.float32)

    def clear_bands(refs):
        @pl.when(b == 0)
        def _():
            for ref in refs:
                ref[low] = zero

        @pl.when(b == bands - 1)
        def _():
            for ref in refs:
                ref[high] = zero

    for copy in loads[4:]:
        copy.wait()
    for copy in y_copies:
        copy.wait_recv()
    clear_bands([wide.at[f] for f in range(7)])

    def look_up(i, carry):
        here = pl.ds(pl.multiple_of(i * 64, 8), 64)
        kind = kinds[here]
        depth = jnp.full((64, LANES), table[0], jnp.float32)
        for c in range(1, table.shape[0]):
            depth = jnp.where(kind == c, table[c], depth)
        wide[7, here] = depth
        return carry

    lax.fori_loop(0, (tile_y + 2 * RIM) // 64, look_up, 0)

    own_x = pl.ds(TOP, tile_x)
    before, after = pl.ds(PAD, RIM), pl.ds(TOP + tile_x, RIM)

    def turned(src, j):
        return src[pl.ds(j, LANES, stride=JS)].T

    def x_exchange(n, ref):
        lead = (slice(None),) * (len(ref.shape) - 2)
        return [
            remote(
                ref.at[lead + (pl.ds(TOP, RIM),)], ref.at[lead + (after,)],
                x_send.at[0, n], x_recv.at[0, n], along_gx(-1),
            ),
            remote(
                ref.at[lead + (pl.ds(TOP + tile_x - RIM, RIM),)], ref.at[lead + (before,)],
                x_send.at[1, n], x_recv.at[1, n], along_gx(1),
            ),
        ]

    x_copies = [x_exchange(n, ref) for n, ref in enumerate((dep, eta, uu, vv))]
    for j in range(JS):
        dep[j, own_x] = turned(wide.at[7], j)
    start(x_copies[0])
    for j in range(JS):
        eta[j, own_x] = turned(wide.at[0], j)
    start(x_copies[1])
    for k in range(3):
        for j in range(JS):
            uu[k, j, own_x] = turned(wide.at[1 + k], j)
    start(x_copies[2])
    for k in range(3):
        for j in range(JS):
            vv[k, j, own_x] = turned(wide.at[4 + k], j)
    start(x_copies[3])
    for n in order[2:]:
        start(rises[n])

    block = ngy * rc
    size = min(block, LANES)
    for j in range(cells_x // LANES):
        value = hm[:, j * LANES : (j + 1) * LANES].T
        for part in range(LANES // size):
            x0 = j * LANES + part * size
            group = x0 // block
            hmt[group // ngx, group % ngx, pl.ds(x0 % block, size)] = value[
                part * size : (part + 1) * size
            ]
    hm_copies = []
    for j in range(1, ngx):
        device = along_gx(j)
        hm_copies.append(
            remote(hmt.at[:, device[1]], rx.at[g], hm_send.at[j], hm_recv.at[j], device)
        )
    hm_copies.append(pltpu.make_async_copy(hmt.at[:, g], rx.at[g], own_sem.at[5]))

    def over_rows(depth, fn):
        lo = (TOP - depth) // 8
        hi = -(-(TOP + tile_x + depth) // 8)
        count = hi - lo
        group = max(u for u in range(1, UNROLL + 1) if count % u == 0)

        def body(i, carry):
            for u in range(group):
                fn(pl.multiple_of((lo + u) * 8 + i * (8 * group), 8))
            return carry

        lax.fori_loop(0, count // group, body, 0)

    def make_mask(r):
        here = pl.ds(r, 8)
        x = r + lax.broadcasted_iota(jnp.int32, (8, LANES), 0)
        columns = ((x >= TOP) | (g > 0)) & ((x < TOP + tile_x) | (g < ngx - 1))
        for j in range(JS):
            at = JS * lane_of((8, LANES)) + j
            band = ((at >= RIM) | (b > 0)) & ((at < RIM + tile_y) | (b < bands - 1))
            mask[j, here] = (columns & band).astype(jnp.float32)

    over_rows(RIM, make_mask)

    def land(n):
        clear_bands([wide_rise.at[n]])
        if n < LEVELS:
            for j in range(JS):
                rt[n, j, own_x] = turned(wide_rise.at[n], j)
            return
        for j in range(JS):
            value = turned(wide_rise.at[n], j)
            for level in range(LEVELS):
                w, at = WINDOW[level], SHIFT[level]
                rt[level, j, pl.ds(TOP - w, w)] = value[at - w : at]
                rt[level, j, pl.ds(TOP + tile_x, w)] = value[at : at + w]

    for i, n in enumerate(order):
        finish_recv(rises[n])
        start(relay[n])
        if i:
            for copy in relay[order[i - 1]]:
                copy.wait_recv()
            land(order[i - 1])
    for copy in relay[order[-1]]:
        copy.wait_recv()
    land(order[-1])

    for pair in x_copies:
        for copy in pair:
            copy.wait()
    start(hm_copies)

    def clear_columns(rows):
        nothing = jnp.zeros((JS, RIM, LANES), jnp.float32)
        eta[:, rows] = nothing
        for k in range(3):
            uu[k, :, rows] = nothing
            vv[k, :, rows] = nothing
        for level in range(LEVELS):
            rt[level, :, rows] = nothing

    @pl.when(g == 0)
    def _():
        clear_columns(before)

    @pl.when(g == ngx - 1)
    def _():
        clear_columns(after)

    def invert(r):
        here = pl.ds(r, 8)
        for j in range(JS):
            depth = dep[j, here]
            scale = mask[j, here] * SPREAD
            k = 9.0 / (depth * depth)
            i1 = 1.0 / (1.0 + 3.0 * k)
            l1 = k * i1
            i2 = 1.0 / (1.0 + 2.0 * k - k * l1)
            l2 = k * i2
            i3 = 1.0 / (1.0 + k - k * l2)
            coef[0, j, here] = l1
            coef[1, j, here] = l2
            coef[2, j, here] = i1 * scale
            coef[3, j, here] = i2 * scale
            coef[4, j, here] = i3 * scale

    over_rows(26, invert)

    def solve(j, here, v):
        l1, l2 = coef[0, j, here], coef[1, j, here]
        y2 = v[1] + l1 * v[0]
        y3 = v[2] + l2 * y2
        x3 = y3 * coef[4, j, here]
        x2 = y2 * coef[3, j, here] + l2 * x3
        x1 = v[0] * coef[2, j, here] + l1 * x2
        return x1, x2, x3

    def ring(ref, here):
        c = [ref[j, here] for j in range(JS)]
        return [turn(c[-1], 1)] + c + [turn(c[0], -1)]

    def predict(depth):
        def rows_of(r):
            here, up, down = pl.ds(r, 8), pl.ds(r + 1, 8), pl.ds(r - 1, 8)
            c = ring(eta, here)
            for j in range(JS):
                push = mask[j, here] * (0.5 * GRAVITY_PUSH)
                ge = push * (eta[j, up] - eta[j, down])
                gn = push * (c[j + 2] - c[j])
                for k in range(3):
                    uu[k, j, here] = uu[k, j, here] - ge
                    vv[k, j, here] = vv[k, j, here] - gn

        over_rows(depth, rows_of)

    def source(depth, level):
        def rows_of(r):
            here, up, down = pl.ds(r, 8), pl.ds(r + 1, 8), pl.ds(r - 1, 8)
            c = [ring(vv.at[k], here) for k in range(3)]
            for j in range(JS):
                rise = rt[level, j, here]
                v = []
                for k in range(3):
                    spread = (uu[k, j, up] - uu[k, j, down]) + (c[k][j + 2] - c[k][j])
                    v.append((4.0 * SOURCE * LAYER_SHARE[k]) * rise - 2.0 * spread)
                    ss[k, j, here] = v[k]
                if level == 0:
                    for k, value in enumerate(solve(j, here, v)):
                        pb[k, j, here] = value

        over_rows(depth, rows_of)

    def sweep(depth, old, new):
        def rows_of(r):
            here, up, down = pl.ds(r, 8), pl.ds(r + 1, 8), pl.ds(r - 1, 8)
            c = [ring(old.at[k], here) for k in range(3)]
            for j in range(JS):
                v = []
                for k in range(3):
                    v.append(
                        (ss[k, j, here] + (c[k][j + 2] + c[k][j]))
                        + (old[k, j, up] + old[k, j, down])
                    )
                for k, value in enumerate(solve(j, here, v)):
                    new[k, j, here] = value

        over_rows(depth, rows_of)

    def correct(depth, level):
        def rows_of(r):
            here, up, down = pl.ds(r, 8), pl.ds(r + 1, 8), pl.ds(r - 1, 8)
            c = [ring(pa.at[k], here) for k in range(3)]
            for j in range(JS):
                push = mask[j, here] * (0.5 * SPREAD)
                for k in range(3):
                    uu[k, j, here] = uu[k, j, here] - push * (pa[k, j, up] - pa[k, j, down])
                    vv[k, j, here] = vv[k, j, here] - push * (c[k][j + 2] - c[k][j])
                low_layer = c[2][j + 1] * (1.0 / LEVELS)
                qq[j, here] = low_layer if level == 0 else qq[j, here] + low_layer

        over_rows(depth, rows_of)

    def raise_surface(depth, level):
        def rows_of(r):
            here, up, down = pl.ds(r, 8), pl.ds(r + 1, 8), pl.ds(r - 1, 8)
            c = [
                vv[0, j, here] + vv[1, j, here] + vv[2, j, here] for j in range(JS)
            ]
            c = [turn(c[-1], 1)] + c + [turn(c[0], -1)]
            for j in range(JS):
                push = mask[j, here] * (0.5 * SURFACE_STEP)
                total = (uu[0, j, up] + uu[1, j, up] + uu[2, j, up]) - (
                    uu[0, j, down] + uu[1, j, down] + uu[2, j, down]
                )
                eta[j, here] = (
                    eta[j, here] - push * (total + (c[j + 2] - c[j])) + rt[level, j, here]
                )

        over_rows(depth, rows_of)

    def step(level):
        rim = 7 * (LEVELS - 1 - level)
        predict(rim + 6)
        source(rim + 5, level)
        if level > 0:
            sweep(rim + 5, pa, pb)
        sweep(rim + 4, pb, pa)
        sweep(rim + 3, pa, pb)
        sweep(rim + 2, pb, pa)
        correct(rim + 1, level)
        raise_surface(rim, level)

    step(0)

    finish_recv(hm_copies)
    lane64 = lane_of((block, LANES)) < 64
    for part in range(nsec):
        for p in range(ngx // 2):
            one, two = rx[2 * p, part], rx[2 * p + 1, part]
            columns = pl.ds(p * LANES, LANES)
            hh[0, part, :, columns] = jnp.where(lane64, one, turn(two, 64))
            hh[1, part, :, columns] = jnp.where(lane64, turn(one, 64), two)
    band_columns = pl.ds(pl.multiple_of(b * tile_y, LANES), tile_y)
    h2_copies = []
    for which, out in enumerate((thick_out, mom_out)):
        for j in range(1, bands):
            device = along_band(j)
            h2_copies.append(
                remote(
                    hh.at[which, device[0], pl.ds(pl.multiple_of(device[2] * rc, 8), rc)],
                    out.at[:, band_columns],
                    h2_send.at[which, j], h2_recv.at[which, j], device,
                )
            )
    for which, out in enumerate((thick_out, mom_out)):
        h2_copies.append(
            pltpu.make_async_copy(
                hh.at[which, s, pl.ds(pl.multiple_of(y * rc, 8), rc)],
                out.at[:, band_columns],
                own_sem.at[6 + which],
            )
        )
    start(h2_copies)

    for level in range(1, LEVELS):
        step(level)

    def turn_back(n, ref):
        for j in range(JS):
            back[n, pl.ds(j, LANES, stride=JS)] = ref[j, own_x].T

    turn_back(4, qq)
    b_copies = []
    columns = pl.ds(pl.multiple_of(g * LANES, LANES), LANES)
    for j in range(1, ngx):
        device = along_gx(j)
        b_copies.append(
            remote(
                back.at[4, strip_rows(device[1])], bottom_out.at[0, 0, :, columns],
                b_send.at[j], b_recv.at[j], device,
            )
        )
    b_copies.append(
        pltpu.make_async_copy(
            back.at[4, strip_rows(g)], bottom_out.at[0, 0, :, columns], own_sem.at[8]
        )
    )
    start(b_copies)
    for k in range(3):
        turn_back(1 + k, pa.at[k])
    turn_back(0, eta)
    outs = [
        pltpu.make_async_copy(back.at[0, own_rows], surf_out, out_sem.at[0]),
        pltpu.make_async_copy(back.at[pl.ds(1, 3), own_rows], press_out, out_sem.at[1]),
    ]
    start(outs)
    finish_recv(b_copies)
    for copy in h2_copies[:-2]:
        copy.wait_recv()
    for copy in h2_copies[-2:] + outs:
        copy.wait()
    for copies in rises + [hm_copies, b_copies]:
        for copy in copies[:-1]:
            copy.wait_send()
    for copies in relay + [y_copies, h2_copies[:-2]]:
        for copy in copies:
            copy.wait_send()


def write_results(*refs):
    count = len(refs) // 2
    sem = refs[-1]
    copies = [
        pltpu.make_async_copy(refs[n], refs[count + n], sem.at[n]) for n in range(count)
    ]
    for copy in copies:
        copy.start()
    for copy in copies:
        copy.wait()


def shards(
    slide_thickness, footprint, slide_momentum, bed_friction, surface, flux_x, flux_y,
    bathy_class, depth_table,
):
    nsec, ngx, ngy = (lax.axis_size(a) for a in ("sec", "gx", "gy"))
    _, _, strip_w, cells_x = slide_thickness.shape
    tile_y, tile_x = surface.shape
    assert tile_x == LANES and strip_w * 2 == LANES and strip_w * ngx == tile_y
    rc = cells_x // (nsec * ngx * ngy)
    bands = nsec * ngy
    x_rows = tile_x + 2 * TOP
    f32 = jnp.float32
    one = (JS, x_rows, LANES)
    three = (3,) + one
    wide_rows = JS * LANES
    results = (
        jax.ShapeDtypeStruct(surface.shape, f32),
        jax.ShapeDtypeStruct(flux_x.shape, f32),
        jax.ShapeDtypeStruct(slide_thickness.shape, f32),
        jax.ShapeDtypeStruct((rc, tile_y * bands), f32),
        jax.ShapeDtypeStruct((rc, tile_y * bands), f32),
    )
    dma = pltpu.SemaphoreType.DMA
    anywhere = pl.BlockSpec(memory_space=pl.ANY)
    made = pl.pallas_call(
        functools.partial(kernel, (nsec, ngx, ngy, tile_y, strip_w, cells_x, rc)),
        out_shape=results,
        in_specs=[anywhere] * 8 + [pl.BlockSpec(memory_space=pltpu.SMEM)],
        out_specs=(anywhere,) * 5,
        scratch_shapes=[
            pltpu.VMEM((3, strip_w, cells_x), f32),
            pltpu.VMEM((strip_w, cells_x), jnp.int32),
            pltpu.VMEM((LEVELS, ngx, strip_w, LANES), f32),
            pltpu.VMEM((ngx, strip_w, LANES), f32),
            pltpu.VMEM((2 * strip_w, cells_x), f32),
            pltpu.VMEM((nsec, ngx, ngy * rc, LANES), f32),
            pltpu.VMEM((ngx, nsec, ngy * rc, LANES), f32),
            pltpu.VMEM((2, nsec, ngy * rc, tile_y), f32),
            pltpu.VMEM((8, wide_rows, LANES), f32),
            pltpu.VMEM((tile_y + 2 * RIM, LANES), jnp.int32),
            pltpu.VMEM((LEVELS + 1, wide_rows, LANES), f32),
            pltpu.VMEM(one, f32),
            pltpu.VMEM(three, f32),
            pltpu.VMEM(three, f32),
            pltpu.VMEM(one, f32),
            pltpu.VMEM(three, f32),
            pltpu.VMEM(three, f32),
            pltpu.VMEM(three, f32),
            pltpu.VMEM((5,) + one, f32),
            pltpu.VMEM(one, f32),
            pltpu.VMEM(one, f32),
            pltpu.VMEM((LEVELS,) + one, f32),
            pltpu.VMEM((5, wide_rows, LANES), f32),
            dma((8,)),
            dma((2,)),
            dma((2, 4)), dma((2, 4)),
            dma((LEVELS + 1, ngx)), dma((LEVELS + 1, ngx)),
            dma((2, LEVELS + 1)), dma((2, LEVELS + 1)),
            dma((2, 4)), dma((2, 4)),
            dma((ngx,)), dma((ngx,)),
            dma((2, bands)), dma((2, bands)),
            dma((ngx,)), dma((ngx,)),
            dma((9,)),
        ],
        compiler_params=pltpu.CompilerParams(
            collective_id=0, has_side_effects=True, vmem_limit_bytes=56 * 2**20
        ),
    )(
        slide_thickness, footprint, slide_momentum, bed_friction, surface, flux_x, flux_y,
        bathy_class, depth_table,
    )
    return pl.pallas_call(
        write_results,
        out_shape=results,
        in_specs=[anywhere] * 5,
        out_specs=(anywhere,) * 5,
        scratch_shapes=[dma((5,))],
    )(*made)


def solution(mesh):
    strips = P(("sec", "gy"), "gx", None, None)
    tiles = P(("sec", "gy"), "gx")
    layers = P(None, ("sec", "gy"), "gx")
    turned = P(("sec", "gx", "gy"), None)
    return jax.shard_map(
        shards,
        mesh=mesh,
        in_specs=(strips,) * 4 + (tiles, layers, layers, tiles, P()),
        out_specs=(tiles, layers, strips, turned, turned),
        check_vma=False,
    )
```

time: 190 us -> 145 us (0.76)
  the two profiles are of different devices: /device:TPU:24 before, /device:TPU:1 now
where the time goes in v2:
time: 145 us
  Pallas kernels  144 us (99%)
    pallas_call x1, Pallas kernels, shards(): pl.pallas_call(functools.partial(kernel, (nsec, ngx, ngy, tile_y, strip_w...  87.5 us
    pallas_call x1, Pallas kernels, shards(): pl.pallas_call(write_results, out_shape=results, in_specs=[anywhere] * 5,...  56.7 us

profile of v2, /device:TPU:1, one launch (start us, length us, event | category | flops | bytes accessed | tf_op | source)
XLA Modules:
  0.0 144.9 jit_solution(462959489418765927)
XLA Ops:
  0.6 87.5 %shard_map.128 = (f32[512,128]{1,0:T(8,128)}, f32[3,512,128]{2,1,0:T(8,128)}, f32[1,1,64,1024]{3,2,1,0:T(8,128)}, f32[8,8192]{1,0:T(8,128)}, f32[8,8192]{1,0:T(8,128)}) custom-call(f32[1,1,64,1024]{3,2,1,0:T(8,128)} %thick_in.1, s32[1,1,64,1024]{3,2,1,0:T(8,128)} %foot_in.1, f32[1,1,64,1024]{3,2,1,0:T(8,128)} %mom_in.1, f32[1,1,64,1024]{3,2,1,0:T(8,128)} %fric_in.1, ...), custom_call_target="tpu_custom_call" | custom-call | tf_op jit(solution)/shard_map/pallas_call | solution.py:607
  88.2 56.7 %shard_map.129 = (f32[512,128]{1,0:T(8,128)}, f32[3,512,128]{2,1,0:T(8,128)}, f32[1,1,64,1024]{3,2,1,0:T(8,128)}, f32[8,8192]{1,0:T(8,128)}, f32[8,8192]{1,0:T(8,128)}) custom-call(f32[512,128]{1,0:T(8,128)} %get-tuple-element.10.refs_0_, f32[3,512,128]{2,1,0:T(8,128)} %get-tuple-element.11.refs_1_, f32[1,1,64,1024]{3,2,1,0:T(8,128)} %get-tuple-element.12.refs_2_, ...), custom_call_target="tpu_custom_call" | custom-call | tf_op jit(solution)/shard_map/pallas_call | solution.py:654

commit v3 on v2

--- a/solution.py
+++ b/solution.py
@@ -20,7 +20,8 @@
 LANES = 128
 JS = 5
 RIM = 32
-UNROLL = 4
+TILE = 32
+UNROLL = 1
 PAD = 8
 TOP = PAD + RIM
 WINDOW = (26, 19, 12, 5)
@@ -157,22 +158,17 @@
 
     pl.semaphore_wait(barrier, len(partners))
 
+    for copy in loads[4:]:
+        copy.wait()
     low, high = pl.ds(0, RIM), pl.ds(RIM + tile_y, RIM)
-    first_rows, last_rows = pl.ds(0, RIM), pl.ds(tile_y - RIM, RIM)
+    first_rows, last_rows = pl.ds(RIM, RIM), pl.ds(tile_y, RIM)
     y_copies = []
-    for n, (src, dst) in enumerate(
-        (
-            (lambda r: surf_in.at[r], lambda r: wide.at[0, r]),
-            (lambda r: fx_in.at[:, r], lambda r: wide.at[pl.ds(1, 3), r]),
-            (lambda r: fy_in.at[:, r], lambda r: wide.at[pl.ds(4, 3), r]),
-            (lambda r: bathy_in.at[r], lambda r: kinds.at[r]),
-        )
-    ):
+    for n, of in enumerate((lambda r: wide.at[pl.ds(0, 7), r], lambda r: kinds.at[r])):
         y_copies.append(
-            remote(src(first_rows), dst(high), ys_send.at[0, n], ys_recv.at[0, n], along_band(-1))
+            remote(of(first_rows), of(high), ys_send.at[0, n], ys_recv.at[0, n], along_band(-1))
         )
         y_copies.append(
-            remote(src(last_rows), dst(low), ys_send.at[1, n], ys_recv.at[1, n], along_band(1))
+            remote(of(last_rows), of(low), ys_send.at[1, n], ys_recv.at[1, n], along_band(1))
         )
     start(y_copies)
 
@@ -210,7 +206,7 @@
             ]
         )
     order = (0, 4, 1, 2, 3)
-    for n in order[:2]:
+    for n in order:
         start(rises[n])
 
     zero = jnp.zeros((RIM, LANES), jnp.float32)
@@ -226,8 +222,6 @@
             for ref in refs:
                 ref[high] = zero
 
-    for copy in loads[4:]:
-        copy.wait()
     for copy in y_copies:
         copy.wait_recv()
     clear_bands([wide.at[f] for f in range(7)])
@@ -249,20 +243,21 @@
     def turned(src, j):
         return src[pl.ds(j, LANES, stride=JS)].T
 
-    def x_exchange(n, ref):
+    def x_exchange(n, ref, depth):
         lead = (slice(None),) * (len(ref.shape) - 2)
         return [
             remote(
-                ref.at[lead + (pl.ds(TOP, RIM),)], ref.at[lead + (after,)],
+                ref.at[lead + (pl.ds(TOP, depth),)], ref.at[lead + (pl.ds(TOP + tile_x, depth),)],
                 x_send.at[0, n], x_recv.at[0, n], along_gx(-1),
             ),
             remote(
-                ref.at[lead + (pl.ds(TOP + tile_x - RIM, RIM),)], ref.at[lead + (before,)],
+                ref.at[lead + (pl.ds(TOP + tile_x - depth, depth),)],
+                ref.at[lead + (pl.ds(TOP - depth, depth),)],
                 x_send.at[1, n], x_recv.at[1, n], along_gx(1),
             ),
         ]
 
-    x_copies = [x_exchange(n, ref) for n, ref in enumerate((dep, eta, uu, vv))]
+    x_copies = [x_exchange(n, *of) for n, of in enumerate(((dep, 26), (eta, 28), (uu, 27), (vv, 26)))]
     for j in range(JS):
         dep[j, own_x] = turned(wide.at[7], j)
     start(x_copies[0])
@@ -277,8 +272,6 @@
         for j in range(JS):
             vv[k, j, own_x] = turned(wide.at[4 + k], j)
     start(x_copies[3])
-    for n in order[2:]:
-        start(rises[n])
 
     block = ngy * rc
     size = min(block, LANES)
@@ -299,24 +292,22 @@
     hm_copies.append(pltpu.make_async_copy(hmt.at[:, g], rx.at[g], own_sem.at[5]))
 
     def over_rows(depth, fn):
-        lo = (TOP - depth) // 8
-        hi = -(-(TOP + tile_x + depth) // 8)
-        count = hi - lo
+        lo = (TOP - depth) // 8 * 8
+        count = -(-(TOP + tile_x + depth - lo) // TILE)
         group = max(u for u in range(1, UNROLL + 1) if count % u == 0)
 
         def body(i, carry):
-            for u in range(group):
-                fn(pl.multiple_of((lo + u) * 8 + i * (8 * group), 8))
+            fn(pl.multiple_of(lo + i * TILE, 8))
             return carry
 
-        lax.fori_loop(0, count // group, body, 0)
+        lax.fori_loop(0, count, body, 0, unroll=group)
 
     def make_mask(r):
-        here = pl.ds(r, 8)
-        x = r + lax.broadcasted_iota(jnp.int32, (8, LANES), 0)
+        here = pl.ds(r, TILE)
+        x = r + lax.broadcasted_iota(jnp.int32, (TILE, LANES), 0)
         columns = ((x >= TOP) | (g > 0)) & ((x < TOP + tile_x) | (g < ngx - 1))
         for j in range(JS):
-            at = JS * lane_of((8, LANES)) + j
+            at = JS * lane_of((TILE, LANES)) + j
             band = ((at >= RIM) | (b > 0)) & ((at < RIM + tile_y) | (b < bands - 1))
             mask[j, here] = (columns & band).astype(jnp.float32)
 
@@ -369,7 +360,7 @@
         clear_columns(after)
 
     def invert(r):
-        here = pl.ds(r, 8)
+        here = pl.ds(r, TILE)
         for j in range(JS):
             depth = dep[j, here]
             scale = mask[j, here] * SPREAD
@@ -402,7 +393,7 @@
 
     def predict(depth):
         def rows_of(r):
-            here, up, down = pl.ds(r, 8), pl.ds(r + 1, 8), pl.ds(r - 1, 8)
+            here, up, down = pl.ds(r, TILE), pl.ds(r + 1, TILE), pl.ds(r - 1, TILE)
             c = ring(eta, here)
             for j in range(JS):
                 push = mask[j, here] * (0.5 * GRAVITY_PUSH)
@@ -416,7 +407,7 @@
 
     def source(depth, level):
         def rows_of(r):
-            here, up, down = pl.ds(r, 8), pl.ds(r + 1, 8), pl.ds(r - 1, 8)
+            here, up, down = pl.ds(r, TILE), pl.ds(r + 1, TILE), pl.ds(r - 1, TILE)
             c = [ring(vv.at[k], here) for k in range(3)]
             for j in range(JS):
                 rise = rt[level, j, here]
@@ -433,7 +424,7 @@
 
     def sweep(depth, old, new):
         def rows_of(r):
-            here, up, down = pl.ds(r, 8), pl.ds(r + 1, 8), pl.ds(r - 1, 8)
+            here, up, down = pl.ds(r, TILE), pl.ds(r + 1, TILE), pl.ds(r - 1, TILE)
             c = [ring(old.at[k], here) for k in range(3)]
             for j in range(JS):
                 v = []
@@ -449,21 +440,22 @@
 
     def correct(depth, level):
         def rows_of(r):
-            here, up, down = pl.ds(r, 8), pl.ds(r + 1, 8), pl.ds(r - 1, 8)
+            here, up, down = pl.ds(r, TILE), pl.ds(r + 1, TILE), pl.ds(r - 1, TILE)
             c = [ring(pa.at[k], here) for k in range(3)]
             for j in range(JS):
                 push = mask[j, here] * (0.5 * SPREAD)
                 for k in range(3):
                     uu[k, j, here] = uu[k, j, here] - push * (pa[k, j, up] - pa[k, j, down])
                     vv[k, j, here] = vv[k, j, here] - push * (c[k][j + 2] - c[k][j])
-                low_layer = c[2][j + 1] * (1.0 / LEVELS)
-                qq[j, here] = low_layer if level == 0 else qq[j, here] + low_layer
+                if level < LEVELS - 1:
+                    low_layer = c[2][j + 1] * (1.0 / LEVELS)
+                    qq[j, here] = low_layer if level == 0 else qq[j, here] + low_layer
 
         over_rows(depth, rows_of)
 
     def raise_surface(depth, level):
         def rows_of(r):
-            here, up, down = pl.ds(r, 8), pl.ds(r + 1, 8), pl.ds(r - 1, 8)
+            here, up, down = pl.ds(r, TILE), pl.ds(r + 1, TILE), pl.ds(r - 1, TILE)
             c = [
                 vv[0, j, here] + vv[1, j, here] + vv[2, j, here] for j in range(JS)
             ]
@@ -479,7 +471,7 @@
 
         over_rows(depth, rows_of)
 
-    def step(level):
+    def begin(level):
         rim = 7 * (LEVELS - 1 - level)
         predict(rim + 6)
         source(rim + 5, level)
@@ -488,10 +480,15 @@
         sweep(rim + 4, pb, pa)
         sweep(rim + 3, pa, pb)
         sweep(rim + 2, pb, pa)
+
+    def step(level):
+        rim = 7 * (LEVELS - 1 - level)
+        begin(level)
         correct(rim + 1, level)
         raise_surface(rim, level)
 
     step(0)
+    step(1)
 
     finish_recv(hm_copies)
     lane64 = lane_of((block, LANES)) < 64
@@ -523,14 +520,17 @@
         )
     start(h2_copies)
 
-    for level in range(1, LEVELS):
-        step(level)
+    step(2)
 
     def turn_back(n, ref):
         for j in range(JS):
             back[n, pl.ds(j, LANES, stride=JS)] = ref[j, own_x].T
 
-    turn_back(4, qq)
+    begin(LEVELS - 1)
+    for j in range(JS):
+        back[4, pl.ds(j, LANES, stride=JS)] = (
+            qq[j, own_x] + pa[2, j, own_x] * (1.0 / LEVELS)
+        ).T
     b_copies = []
     columns = pl.ds(pl.multiple_of(g * LANES, LANES), LANES)
     for j in range(1, ngx):
@@ -547,14 +547,17 @@
         )
     )
     start(b_copies)
+    correct(1, LEVELS - 1)
     for k in range(3):
         turn_back(1 + k, pa.at[k])
+    outs = [
+        pltpu.make_async_copy(back.at[pl.ds(1, 3), own_rows], press_out, out_sem.at[1]),
+        pltpu.make_async_copy(back.at[0, own_rows], surf_out, out_sem.at[0]),
+    ]
+    outs[0].start()
+    raise_surface(0, LEVELS - 1)
     turn_back(0, eta)
-    outs = [
-        pltpu.make_async_copy(back.at[0, own_rows], surf_out, out_sem.at[0]),
-        pltpu.make_async_copy(back.at[pl.ds(1, 3), own_rows], press_out, out_sem.at[1]),
-    ]
-    start(outs)
+    outs[1].start()
     finish_recv(b_copies)
     for copy in h2_copies[:-2]:
         copy.wait_recv()
@@ -569,14 +572,17 @@
 
 
 def write_results(*refs):
-    count = len(refs) // 2
-    sem = refs[-1]
-    copies = [
-        pltpu.make_async_copy(refs[n], refs[count + n], sem.at[n]) for n in range(count)
-    ]
-    for copy in copies:
+    count = (len(refs) - 2) // 3
+    given, results, held = refs[:count], refs[count : 2 * count], refs[2 * count : 3 * count]
+    in_sem, out_sem = refs[3 * count :]
+    ins = [pltpu.make_async_copy(given[n], held[n], in_sem.at[n]) for n in range(count)]
+    outs = [pltpu.make_async_copy(held[n], results[n], out_sem.at[n]) for n in range(count)]
+    for copy in ins:
         copy.start()
-    for copy in copies:
+    for n in range(count):
+        ins[n].wait()
+        outs[n].start()
+    for copy in outs:
         copy.wait()
 
 
@@ -590,7 +596,7 @@
     assert tile_x == LANES and strip_w * 2 == LANES and strip_w * ngx == tile_y
     rc = cells_x // (nsec * ngx * ngy)
     bands = nsec * ngy
-    x_rows = tile_x + 2 * TOP
+    x_rows = tile_x + 2 * TOP + 16
     f32 = jnp.float32
     one = (JS, x_rows, LANES)
     three = (3,) + one
@@ -656,7 +662,7 @@
         out_shape=results,
         in_specs=[anywhere] * 5,
         out_specs=(anywhere,) * 5,
-        scratch_shapes=[dma((5,))],
+        scratch_shapes=[pltpu.VMEM(r.shape, f32) for r in results] + [dma((5,)), dma((5,))],
     )(*made)
 
 

time: 145 us -> 78.6 us (0.54)
  Pallas kernels: 144 us -> 77.8 us
    pallas_call x1, Pallas kernels: 56.7 us -> 2.44 us  [shards(): pl.pallas_call(write_results, out_shape=results, in_specs=[anywhere] * 5,...]
    pallas_call x1, Pallas kernels: 87.5 us -> 75.3 us  [shards(): pl.pallas_call(functools.partial(kernel, (nsec, ngx, ngy, tile_y, strip_w...]
where the time goes in v3:
time: 78.6 us; the launch traced here: 78.4 us
  Pallas kernels  77.8 us (99%)
    pallas_call x1, Pallas kernels, shards(): pl.pallas_call(functools.partial(kernel, (nsec, ngx, ngy, tile_y, strip_w...  75.3 us
    pallas_call x1, Pallas kernels, shards(): pl.pallas_call(write_results, out_shape=results, in_specs=[anywhere] * 5,...  2.44 us

profile of v3, /device:TPU:1, one launch (start us, length us, event | category | flops | bytes accessed | tf_op | source)
XLA Modules:
  0.0 78.4 jit_solution(1232572521399028825)
XLA Ops:
  0.6 75.3 %shard_map.128 = (f32[512,128]{1,0:T(8,128)}, f32[3,512,128]{2,1,0:T(8,128)}, f32[1,1,64,1024]{3,2,1,0:T(8,128)}, f32[8,8192]{1,0:T(8,128)}, f32[8,8192]{1,0:T(8,128)}) custom-call(f32[1,1,64,1024]{3,2,1,0:T(8,128)} %thick_in.1, s32[1,1,64,1024]{3,2,1,0:T(8,128)} %foot_in.1, f32[1,1,64,1024]{3,2,1,0:T(8,128)} %mom_in.1, f32[1,1,64,1024]{3,2,1,0:T(8,128)} %fric_in.1, ...), custom_call_target="tpu_custom_call" | custom-call | tf_op jit(solution)/shard_map/pallas_call | solution.py:613
  76.0 2.4 %shard_map.129 = (f32[512,128]{1,0:T(8,128)}, f32[3,512,128]{2,1,0:T(8,128)}, f32[1,1,64,1024]{3,2,1,0:T(8,128)}, f32[8,8192]{1,0:T(8,128)}, f32[8,8192]{1,0:T(8,128)}) custom-call(f32[512,128]{1,0:T(8,128)} %get-tuple-element.10.refs_0_, f32[3,512,128]{2,1,0:T(8,128)} %get-tuple-element.11.refs_1_, f32[1,1,64,1024]{3,2,1,0:T(8,128)} %get-tuple-element.12.refs_2_, ...), custom_call_target="tpu_custom_call" | custom-call | tf_op jit(solution)/shard_map/pallas_call | solution.py:660

commit v4 on v3

--- a/solution.py
+++ b/solution.py
@@ -25,6 +25,7 @@
 PAD = 8
 TOP = PAD + RIM
 WINDOW = (26, 19, 12, 5)
+X_AFTER = {0: (0, 1), 2: (2,), 4: (3,)}
 SHIFT = (26, 71, 102, 119)
 
 
@@ -92,6 +93,23 @@
         for copy in copies:
             copy.start()
 
+    def to_neighbours(at, count, pairs, what):
+        @pl.when(at > 0)
+        def _():
+            for pair in pairs:
+                if what == "recv":
+                    pair[1].wait_recv()
+                else:
+                    pair[0].start() if what == "start" else pair[0].wait_send()
+
+        @pl.when(at < count - 1)
+        def _():
+            for pair in pairs:
+                if what == "recv":
+                    pair[0].wait_recv()
+                else:
+                    pair[1].start() if what == "start" else pair[1].wait_send()
+
     def finish_recv(copies):
         for copy in copies[:-1]:
             copy.wait_recv()
@@ -135,6 +153,59 @@
         return carry
 
     lax.fori_loop(0, strip_w // 8, slide_rows, 0)
+
+    pl.semaphore_wait(barrier, len(partners))
+
+    for copy in loads[4:]:
+        copy.wait()
+    low, high = pl.ds(0, RIM), pl.ds(RIM + tile_y, RIM)
+    first_rows, last_rows = pl.ds(RIM, RIM), pl.ds(tile_y, RIM)
+    y_copies = []
+    for n, of in enumerate((lambda r: wide.at[pl.ds(0, 7), r], lambda r: kinds.at[r])):
+        y_copies.append(
+            (
+                remote(of(first_rows), of(high), ys_send.at[0, n], ys_recv.at[0, n], along_band(-1)),
+                remote(of(last_rows), of(low), ys_send.at[1, n], ys_recv.at[1, n], along_band(1)),
+            )
+        )
+    to_neighbours(b, bands, y_copies, "start")
+
+    def strip_rows(j):
+        return pl.ds(pl.multiple_of(RIM + j * strip_w, 8), strip_w)
+
+    def rise_copies(n, src):
+        copies = []
+        for j in range(1, ngx):
+            device = along_gx(j)
+            copies.append(
+                remote(
+                    src(device[1]), wide_rise.at[n, strip_rows(g)],
+                    rise_send.at[n, j], rise_recv.at[n, j], device,
+                )
+            )
+        own = pltpu.make_async_copy(src(g), wide_rise.at[n, strip_rows(g)], own_sem.at[n])
+        return copies + [own]
+
+    rises = [rise_copies(n, lambda j, n=n: rise_s.at[n, j]) for n in range(LEVELS)]
+    rises.append(rise_copies(LEVELS, lambda j: pack_s.at[j]))
+    relay = []
+    for n in range(LEVELS + 1):
+        ref = wide_rise.at[n]
+        relay.append(
+            [
+                remote(
+                    ref.at[pl.ds(RIM, RIM)], ref.at[high],
+                    rl_send.at[0, n], rl_recv.at[0, n], along_band(-1),
+                ),
+                remote(
+                    ref.at[pl.ds(tile_y, RIM)], ref.at[low],
+                    rl_send.at[1, n], rl_recv.at[1, n], along_band(1),
+                ),
+            ]
+        )
+    order = (0, 1, 4, 2, 3)
+    start(rises[0])
+    start(rises[1])
 
     def pack_rows(i, carry):
         r = pl.ds(pl.multiple_of(i * 16, 16), 16)
@@ -155,58 +226,7 @@
         return carry
 
     lax.fori_loop(0, strip_w // 16, pack_rows, 0)
-
-    pl.semaphore_wait(barrier, len(partners))
-
-    for copy in loads[4:]:
-        copy.wait()
-    low, high = pl.ds(0, RIM), pl.ds(RIM + tile_y, RIM)
-    first_rows, last_rows = pl.ds(RIM, RIM), pl.ds(tile_y, RIM)
-    y_copies = []
-    for n, of in enumerate((lambda r: wide.at[pl.ds(0, 7), r], lambda r: kinds.at[r])):
-        y_copies.append(
-            remote(of(first_rows), of(high), ys_send.at[0, n], ys_recv.at[0, n], along_band(-1))
-        )
-        y_copies.append(
-            remote(of(last_rows), of(low), ys_send.at[1, n], ys_recv.at[1, n], along_band(1))
-        )
-    start(y_copies)
-
-    def strip_rows(j):
-        return pl.ds(pl.multiple_of(RIM + j * strip_w, 8), strip_w)
-
-    def rise_copies(n, src):
-        copies = []
-        for j in range(1, ngx):
-            device = along_gx(j)
-            copies.append(
-                remote(
-                    src(device[1]), wide_rise.at[n, strip_rows(g)],
-                    rise_send.at[n, j], rise_recv.at[n, j], device,
-                )
-            )
-        own = pltpu.make_async_copy(src(g), wide_rise.at[n, strip_rows(g)], own_sem.at[n])
-        return copies + [own]
-
-    rises = [rise_copies(n, lambda j, n=n: rise_s.at[n, j]) for n in range(LEVELS)]
-    rises.append(rise_copies(LEVELS, lambda j: pack_s.at[j]))
-    relay = []
-    for n in range(LEVELS + 1):
-        ref = wide_rise.at[n]
-        relay.append(
-            [
-                remote(
-                    ref.at[pl.ds(RIM, RIM)], ref.at[high],
-                    rl_send.at[0, n], rl_recv.at[0, n], along_band(-1),
-                ),
-                remote(
-                    ref.at[pl.ds(tile_y, RIM)], ref.at[low],
-                    rl_send.at[1, n], rl_recv.at[1, n], along_band(1),
-                ),
-            ]
-        )
-    order = (0, 4, 1, 2, 3)
-    for n in order:
+    for n in (4, 2, 3):
         start(rises[n])
 
     zero = jnp.zeros((RIM, LANES), jnp.float32)
@@ -222,8 +242,7 @@
             for ref in refs:
                 ref[high] = zero
 
-    for copy in y_copies:
-        copy.wait_recv()
+    to_neighbours(b, bands, y_copies, "recv")
     clear_bands([wide.at[f] for f in range(7)])
 
     def look_up(i, carry):
@@ -260,18 +279,14 @@
     x_copies = [x_exchange(n, *of) for n, of in enumerate(((dep, 26), (eta, 28), (uu, 27), (vv, 26)))]
     for j in range(JS):
         dep[j, own_x] = turned(wide.at[7], j)
-    start(x_copies[0])
     for j in range(JS):
         eta[j, own_x] = turned(wide.at[0], j)
-    start(x_copies[1])
     for k in range(3):
         for j in range(JS):
             uu[k, j, own_x] = turned(wide.at[1 + k], j)
-    start(x_copies[2])
     for k in range(3):
         for j in range(JS):
             vv[k, j, own_x] = turned(wide.at[4 + k], j)
-    start(x_copies[3])
 
     block = ngy * rc
     size = min(block, LANES)
@@ -328,22 +343,20 @@
 
     for i, n in enumerate(order):
         finish_recv(rises[n])
-        start(relay[n])
-        if i:
-            for copy in relay[order[i - 1]]:
-                copy.wait_recv()
-            land(order[i - 1])
-    for copy in relay[order[-1]]:
-        copy.wait_recv()
-    land(order[-1])
-
-    for pair in x_copies:
-        for copy in pair:
-            copy.wait()
+        to_neighbours(b, bands, [relay[n]], "start")
+        if i in X_AFTER:
+            to_neighbours(g, ngx, [x_copies[m] for m in X_AFTER[i]], "start")
+    for n in order:
+        to_neighbours(b, bands, [relay[n]], "recv")
+        land(n)
+
+    to_neighbours(g, ngx, x_copies, "recv")
+    to_neighbours(g, ngx, x_copies, "sent")
     start(hm_copies)
 
     def clear_columns(rows):
         nothing = jnp.zeros((JS, RIM, LANES), jnp.float32)
+        dep[:, rows] = nothing + 1.0
         eta[:, rows] = nothing
         for k in range(3):
             uu[k, :, rows] = nothing
@@ -566,9 +579,9 @@
     for copies in rises + [hm_copies, b_copies]:
         for copy in copies[:-1]:
             copy.wait_send()
-    for copies in relay + [y_copies, h2_copies[:-2]]:
-        for copy in copies:
-            copy.wait_send()
+    to_neighbours(b, bands, relay + y_copies, "sent")
+    for copy in h2_copies[:-2]:
+        copy.wait_send()
 
 
 def write_results(*refs):

time: 78.6 us -> 70.2 us (0.89)
  the two profiles are of different devices: /device:TPU:1 before, /device:TPU:24 now
where the time goes in v4:
time: 70.2 us; the launch traced here: 70.1 us
  Pallas kernels  69.4 us (99%)
    pallas_call x1, Pallas kernels, shards(): pl.pallas_call(functools.partial(kernel, (nsec, ngx, ngy, tile_y, strip_w...  67 us
    pallas_call x1, Pallas kernels, shards(): pl.pallas_call(write_results, out_shape=results, in_specs=[anywhere] * 5,...  2.44 us

profile of v4, /device:TPU:24, one launch (start us, length us, event | category | flops | bytes accessed | tf_op | source)
XLA Modules:
  0.0 70.1 jit_solution(5165172628500611638)
XLA Ops:
  0.6 67.0 %shard_map.128 = (f32[512,128]{1,0:T(8,128)}, f32[3,512,128]{2,1,0:T(8,128)}, f32[1,1,64,1024]{3,2,1,0:T(8,128)}, f32[8,8192]{1,0:T(8,128)}, f32[8,8192]{1,0:T(8,128)}) custom-call(f32[1,1,64,1024]{3,2,1,0:T(8,128)} %thick_in.1, s32[1,1,64,1024]{3,2,1,0:T(8,128)} %foot_in.1, f32[1,1,64,1024]{3,2,1,0:T(8,128)} %mom_in.1, f32[1,1,64,1024]{3,2,1,0:T(8,128)} %fric_in.1, ...), custom_call_target="tpu_custom_call" | custom-call | tf_op jit(solution)/shard_map/pallas_call | solution.py:626
  67.6 2.4 %shard_map.129 = (f32[512,128]{1,0:T(8,128)}, f32[3,512,128]{2,1,0:T(8,128)}, f32[1,1,64,1024]{3,2,1,0:T(8,128)}, f32[8,8192]{1,0:T(8,128)}, f32[8,8192]{1,0:T(8,128)}) custom-call(f32[512,128]{1,0:T(8,128)} %get-tuple-element.10.refs_0_, f32[3,512,128]{2,1,0:T(8,128)} %get-tuple-element.11.refs_1_, f32[1,1,64,1024]{3,2,1,0:T(8,128)} %get-tuple-element.12.refs_2_, ...), custom_call_target="tpu_custom_call" | custom-call | tf_op jit(solution)/shard_map/pallas_call | solution.py:673

commit v5 on v4

--- a/solution.py
+++ b/solution.py
@@ -20,8 +20,7 @@
 LANES = 128
 JS = 5
 RIM = 32
-TILE = 32
-UNROLL = 1
+TILE = 64
 PAD = 8
 TOP = PAD + RIM
 WINDOW = (26, 19, 12, 5)
@@ -66,7 +65,7 @@
     surf_out, press_out, bottom_out, thick_out, mom_out,
     sl, foot, rise_s, pack_s, hm, hmt, rx, hh,
     wide, kinds, wide_rise,
-    eta, uu, vv, dep, pa, pb, ss, coef, mask, qq, rt, back,
+    xd, xe, xu, xv, eta, uu, vv, dep, pa, pb, ss, coef, mask, qq, rt, back,
     load_sem, out_sem, ys_send, ys_recv, rise_send, rise_recv, rl_send, rl_recv,
     x_send, x_recv, hm_send, hm_recv, h2_send, h2_recv, b_send, b_recv, own_sem,
 ):
@@ -114,6 +113,11 @@
         for copy in copies[:-1]:
             copy.wait_recv()
         copies[-1].wait()
+
+    barrier = pltpu.get_barrier_semaphore()
+    partners = [along_gx(j) for j in range(1, ngx)] + [along_band(j) for j in range(1, bands)]
+    for device in partners:
+        pl.semaphore_signal(barrier, inc=1, device_id=device, device_id_type=pl.DeviceIdType.MESH)
 
     own_rows = pl.ds(RIM, tile_y)
     loads = [
@@ -127,11 +131,6 @@
         pltpu.make_async_copy(bathy_in, kinds.at[own_rows], load_sem.at[7]),
     ]
     start(loads)
-
-    barrier = pltpu.get_barrier_semaphore()
-    partners = [along_gx(j) for j in range(1, ngx)] + [along_band(j) for j in range(1, bands)]
-    for device in partners:
-        pl.semaphore_signal(barrier, inc=1, device_id=device, device_id_type=pl.DeviceIdType.MESH)
 
     for copy in loads[:4]:
         copy.wait()
@@ -262,31 +261,37 @@
     def turned(src, j):
         return src[pl.ds(j, LANES, stride=JS)].T
 
-    def x_exchange(n, ref, depth):
+    def x_exchange(n, kept, ref, depth):
         lead = (slice(None),) * (len(ref.shape) - 2)
-        return [
+        return (
             remote(
-                ref.at[lead + (pl.ds(TOP, depth),)], ref.at[lead + (pl.ds(TOP + tile_x, depth),)],
+                kept.at[(0,) + lead + (pl.ds(0, depth),)],
+                ref.at[lead + (pl.ds(TOP + tile_x, depth),)],
                 x_send.at[0, n], x_recv.at[0, n], along_gx(-1),
             ),
             remote(
-                ref.at[lead + (pl.ds(TOP + tile_x - depth, depth),)],
+                kept.at[(1,) + lead + (pl.ds(RIM - depth, depth),)],
                 ref.at[lead + (pl.ds(TOP - depth, depth),)],
                 x_send.at[1, n], x_recv.at[1, n], along_gx(1),
             ),
-        ]
-
-    x_copies = [x_exchange(n, *of) for n, of in enumerate(((dep, 26), (eta, 28), (uu, 27), (vv, 26)))]
+        )
+
+    x_copies = [
+        x_exchange(n, *of)
+        for n, of in enumerate(((xd, dep, 26), (xe, eta, 28), (xu, uu, 27), (xv, vv, 26)))
+    ]
     for j in range(JS):
-        dep[j, own_x] = turned(wide.at[7], j)
-    for j in range(JS):
-        eta[j, own_x] = turned(wide.at[0], j)
-    for k in range(3):
-        for j in range(JS):
-            uu[k, j, own_x] = turned(wide.at[1 + k], j)
-    for k in range(3):
-        for j in range(JS):
-            vv[k, j, own_x] = turned(wide.at[4 + k], j)
+        for f, kept, ref in ((7, xd, dep), (0, xe, eta)):
+            value = turned(wide.at[f], j)
+            ref[j, own_x] = value
+            kept[0, j] = value[:RIM]
+            kept[1, j] = value[tile_x - RIM :]
+        for k in range(3):
+            for f, kept, ref in ((1 + k, xu, uu), (4 + k, xv, vv)):
+                value = turned(wide.at[f], j)
+                ref[k, j, own_x] = value
+                kept[0, k, j] = value[:RIM]
+                kept[1, k, j] = value[tile_x - RIM :]
 
     block = ngy * rc
     size = min(block, LANES)
@@ -306,23 +311,36 @@
         )
     hm_copies.append(pltpu.make_async_copy(hmt.at[:, g], rx.at[g], own_sem.at[5]))
 
-    def over_rows(depth, fn):
-        lo = (TOP - depth) // 8 * 8
-        count = -(-(TOP + tile_x + depth - lo) // TILE)
-        group = max(u for u in range(1, UNROLL + 1) if count % u == 0)
+    def over_rows(depth, fn, part=None, inner=0):
+        lo = TOP - depth
+        if part is None:
+            lo = lo // 8 * 8
+            tile, stride = TILE, TILE
+            count = -(-(TOP + tile_x + depth - lo) // TILE)
+        elif part == "inner":
+            lo = TOP + inner
+            count = 2
+            tile = stride = tile_x // 2 - inner
+        else:
+            count = 2
+            tile = depth + inner
+            stride = tile_x - inner + depth
 
         def body(i, carry):
-            fn(pl.multiple_of(lo + i * TILE, 8))
+            start_row = lo + i * stride
+            if part is None:
+                start_row = pl.multiple_of(start_row, 8)
+            fn(start_row, tile)
             return carry
 
-        lax.fori_loop(0, count, body, 0, unroll=group)
-
-    def make_mask(r):
-        here = pl.ds(r, TILE)
-        x = r + lax.broadcasted_iota(jnp.int32, (TILE, LANES), 0)
+        lax.fori_loop(0, count, body, 0)
+
+    def make_mask(r, tile):
+        here = pl.ds(r, tile)
+        x = r + lax.broadcasted_iota(jnp.int32, (tile, LANES), 0)
         columns = ((x >= TOP) | (g > 0)) & ((x < TOP + tile_x) | (g < ngx - 1))
         for j in range(JS):
-            at = JS * lane_of((TILE, LANES)) + j
+            at = JS * lane_of((tile, LANES)) + j
             band = ((at >= RIM) | (b > 0)) & ((at < RIM + tile_y) | (b < bands - 1))
             mask[j, here] = (columns & band).astype(jnp.float32)
 
@@ -350,30 +368,18 @@
         to_neighbours(b, bands, [relay[n]], "recv")
         land(n)
 
-    to_neighbours(g, ngx, x_copies, "recv")
-    to_neighbours(g, ngx, x_copies, "sent")
-    start(hm_copies)
-
-    def clear_columns(rows):
-        nothing = jnp.zeros((JS, RIM, LANES), jnp.float32)
-        dep[:, rows] = nothing + 1.0
-        eta[:, rows] = nothing
-        for k in range(3):
-            uu[k, :, rows] = nothing
-            vv[k, :, rows] = nothing
-        for level in range(LEVELS):
-            rt[level, :, rows] = nothing
+    to_neighbours(g, ngx, x_copies[:1], "recv")
 
     @pl.when(g == 0)
     def _():
-        clear_columns(before)
+        dep[:, before] = jnp.ones((JS, RIM, LANES), jnp.float32)
 
     @pl.when(g == ngx - 1)
     def _():
-        clear_columns(after)
-
-    def invert(r):
-        here = pl.ds(r, TILE)
+        dep[:, after] = jnp.ones((JS, RIM, LANES), jnp.float32)
+
+    def invert(r, tile):
+        here = pl.ds(r, tile)
         for j in range(JS):
             depth = dep[j, here]
             scale = mask[j, here] * SPREAD
@@ -391,6 +397,7 @@
 
     over_rows(26, invert)
 
+
     def solve(j, here, v):
         l1, l2 = coef[0, j, here], coef[1, j, here]
         y2 = v[1] + l1 * v[0]
@@ -404,9 +411,9 @@
         c = [ref[j, here] for j in range(JS)]
         return [turn(c[-1], 1)] + c + [turn(c[0], -1)]
 
-    def predict(depth):
-        def rows_of(r):
-            here, up, down = pl.ds(r, TILE), pl.ds(r + 1, TILE), pl.ds(r - 1, TILE)
+    def predict(depth, *part):
+        def rows_of(r, tile):
+            here, up, down = pl.ds(r, tile), pl.ds(r + 1, tile), pl.ds(r - 1, tile)
             c = ring(eta, here)
             for j in range(JS):
                 push = mask[j, here] * (0.5 * GRAVITY_PUSH)
@@ -416,11 +423,11 @@
                     uu[k, j, here] = uu[k, j, here] - ge
                     vv[k, j, here] = vv[k, j, here] - gn
 
-        over_rows(depth, rows_of)
-
-    def source(depth, level):
-        def rows_of(r):
-            here, up, down = pl.ds(r, TILE), pl.ds(r + 1, TILE), pl.ds(r - 1, TILE)
+        over_rows(depth, rows_of, *part)
+
+    def source(depth, level, *part):
+        def rows_of(r, tile):
+            here, up, down = pl.ds(r, tile), pl.ds(r + 1, tile), pl.ds(r - 1, tile)
             c = [ring(vv.at[k], here) for k in range(3)]
             for j in range(JS):
                 rise = rt[level, j, here]
@@ -433,11 +440,11 @@
                     for k, value in enumerate(solve(j, here, v)):
                         pb[k, j, here] = value
 
-        over_rows(depth, rows_of)
-
-    def sweep(depth, old, new):
-        def rows_of(r):
-            here, up, down = pl.ds(r, TILE), pl.ds(r + 1, TILE), pl.ds(r - 1, TILE)
+        over_rows(depth, rows_of, *part)
+
+    def sweep(depth, old, new, *part):
+        def rows_of(r, tile):
+            here, up, down = pl.ds(r, tile), pl.ds(r + 1, tile), pl.ds(r - 1, tile)
             c = [ring(old.at[k], here) for k in range(3)]
             for j in range(JS):
                 v = []
@@ -449,11 +456,11 @@
                 for k, value in enumerate(solve(j, here, v)):
                     new[k, j, here] = value
 
-        over_rows(depth, rows_of)
-
-    def correct(depth, level):
-        def rows_of(r):
-            here, up, down = pl.ds(r, TILE), pl.ds(r + 1, TILE), pl.ds(r - 1, TILE)
+        over_rows(depth, rows_of, *part)
+
+    def correct(depth, level, *part):
+        def rows_of(r, tile):
+            here, up, down = pl.ds(r, tile), pl.ds(r + 1, tile), pl.ds(r - 1, tile)
             c = [ring(pa.at[k], here) for k in range(3)]
             for j in range(JS):
                 push = mask[j, here] * (0.5 * SPREAD)
@@ -464,11 +471,11 @@
                     low_layer = c[2][j + 1] * (1.0 / LEVELS)
                     qq[j, here] = low_layer if level == 0 else qq[j, here] + low_layer
 
-        over_rows(depth, rows_of)
-
-    def raise_surface(depth, level):
-        def rows_of(r):
-            here, up, down = pl.ds(r, TILE), pl.ds(r + 1, TILE), pl.ds(r - 1, TILE)
+        over_rows(depth, rows_of, *part)
+
+    def raise_surface(depth, level, *part):
+        def rows_of(r, tile):
+            here, up, down = pl.ds(r, tile), pl.ds(r + 1, tile), pl.ds(r - 1, tile)
             c = [
                 vv[0, j, here] + vv[1, j, here] + vv[2, j, here] for j in range(JS)
             ]
@@ -482,26 +489,51 @@
                     eta[j, here] - push * (total + (c[j + 2] - c[j])) + rt[level, j, here]
                 )
 
-        over_rows(depth, rows_of)
-
-    def begin(level):
+        over_rows(depth, rows_of, *part)
+
+    def begin(level, part=None):
         rim = 7 * (LEVELS - 1 - level)
-        predict(rim + 6)
-        source(rim + 5, level)
+        at = 7 * level + 1
+        predict(rim + 6, part, at)
+        source(rim + 5, level, part, at + 1)
         if level > 0:
-            sweep(rim + 5, pa, pb)
-        sweep(rim + 4, pb, pa)
-        sweep(rim + 3, pa, pb)
-        sweep(rim + 2, pb, pa)
-
-    def step(level):
+            sweep(rim + 5, pa, pb, part, at + 1)
+        sweep(rim + 4, pb, pa, part, at + 2)
+        sweep(rim + 3, pa, pb, part, at + 3)
+        sweep(rim + 2, pb, pa, part, at + 4)
+
+    def step(level, part=None):
         rim = 7 * (LEVELS - 1 - level)
-        begin(level)
-        correct(rim + 1, level)
-        raise_surface(rim, level)
-
-    step(0)
-    step(1)
+        at = 7 * level + 1
+        begin(level, part)
+        correct(rim + 1, level, part, at + 5)
+        raise_surface(rim, level, part, at + 6)
+
+    for level in range(2):
+        step(level, "inner")
+    to_neighbours(g, ngx, x_copies[1:], "recv")
+    start(hm_copies)
+
+    def clear_columns(rows):
+        nothing = jnp.zeros((JS, RIM, LANES), jnp.float32)
+        eta[:, rows] = nothing
+        for k in range(3):
+            uu[k, :, rows] = nothing
+            vv[k, :, rows] = nothing
+        for level in range(LEVELS):
+            rt[level, :, rows] = nothing
+
+    @pl.when(g == 0)
+    def _():
+        clear_columns(before)
+
+    @pl.when(g == ngx - 1)
+    def _():
+        clear_columns(after)
+    for level in range(2):
+        step(level, "outer")
+
+    step(2)
 
     finish_recv(hm_copies)
     lane64 = lane_of((block, LANES)) < 64
@@ -532,8 +564,6 @@
             )
         )
     start(h2_copies)
-
-    step(2)
 
     def turn_back(n, ref):
         for j in range(JS):
@@ -580,6 +610,7 @@
         for copy in copies[:-1]:
             copy.wait_send()
     to_neighbours(b, bands, relay + y_copies, "sent")
+    to_neighbours(g, ngx, x_copies, "sent")
     for copy in h2_copies[:-2]:
         copy.wait_send()
 
@@ -609,7 +640,7 @@
     assert tile_x == LANES and strip_w * 2 == LANES and strip_w * ngx == tile_y
     rc = cells_x // (nsec * ngx * ngy)
     bands = nsec * ngy
-    x_rows = tile_x + 2 * TOP + 16
+    x_rows = tile_x + 2 * TOP + 48
     f32 = jnp.float32
     one = (JS, x_rows, LANES)
     three = (3,) + one
@@ -640,6 +671,10 @@
             pltpu.VMEM((8, wide_rows, LANES), f32),
             pltpu.VMEM((tile_y + 2 * RIM, LANES), jnp.int32),
             pltpu.VMEM((LEVELS + 1, wide_rows, LANES), f32),
+            pltpu.VMEM((2, JS, RIM, LANES), f32),
+            pltpu.VMEM((2, JS, RIM, LANES), f32),
+            pltpu.VMEM((2, 3, JS, RIM, LANES), f32),
+            pltpu.VMEM((2, 3, JS, RIM, LANES), f32),
             pltpu.VMEM(one, f32),
             pltpu.VMEM(three, f32),
             pltpu.VMEM(three, f32),

time: 70.2 us -> 65.9 us (0.939); the launches traced: 70.1 us -> 65 us
  Pallas kernels: 69.4 us -> 64.4 us
    pallas_call x1, Pallas kernels: 67 us -> 61.9 us  [shards(): pl.pallas_call(functools.partial(kernel, (nsec, ngx, ngy, tile_y, strip_w...]
where the time goes in v5:
time: 65.9 us; the launch traced here: 65 us
  Pallas kernels  64.4 us (98%)
    pallas_call x1, Pallas kernels, shards(): pl.pallas_call(functools.partial(kernel, (nsec, ngx, ngy, tile_y, strip_w...  61.9 us
    pallas_call x1, Pallas kernels, shards(): pl.pallas_call(write_results, out_shape=results, in_specs=[anywhere] * 5,...  2.44 us

profile of v5, /device:TPU:24, one launch (start us, length us, event | category | flops | bytes accessed | tf_op | source)
XLA Modules:
  0.0 65.0 jit_solution(12740941296410422215)
XLA Ops:
  0.6 61.9 %shard_map.128 = (f32[512,128]{1,0:T(8,128)}, f32[3,512,128]{2,1,0:T(8,128)}, f32[1,1,64,1024]{3,2,1,0:T(8,128)}, f32[8,8192]{1,0:T(8,128)}, f32[8,8192]{1,0:T(8,128)}) custom-call(f32[1,1,64,1024]{3,2,1,0:T(8,128)} %thick_in.1, s32[1,1,64,1024]{3,2,1,0:T(8,128)} %foot_in.1, f32[1,1,64,1024]{3,2,1,0:T(8,128)} %mom_in.1, f32[1,1,64,1024]{3,2,1,0:T(8,128)} %fric_in.1, ...), custom_call_target="tpu_custom_call" | custom-call | tf_op jit(solution)/shard_map/pallas_call | solution.py:657
  62.6 2.4 %shard_map.129 = (f32[512,128]{1,0:T(8,128)}, f32[3,512,128]{2,1,0:T(8,128)}, f32[1,1,64,1024]{3,2,1,0:T(8,128)}, f32[8,8192]{1,0:T(8,128)}, f32[8,8192]{1,0:T(8,128)}) custom-call(f32[512,128]{1,0:T(8,128)} %get-tuple-element.10.refs_0_, f32[3,512,128]{2,1,0:T(8,128)} %get-tuple-element.11.refs_1_, f32[1,1,64,1024]{3,2,1,0:T(8,128)} %get-tuple-element.12.refs_2_, ...), custom_call_target="tpu_custom_call" | custom-call | tf_op jit(solution)/shard_map/pallas_call | solution.py:708

commit v6 on v5

--- a/solution.py
+++ b/solution.py
@@ -509,10 +509,10 @@
         correct(rim + 1, level, part, at + 5)
         raise_surface(rim, level, part, at + 6)
 
-    for level in range(2):
-        step(level, "inner")
+    step(0, "inner")
+    start(hm_copies)
+    step(1, "inner")
     to_neighbours(g, ngx, x_copies[1:], "recv")
-    start(hm_copies)
 
     def clear_columns(rows):
         nothing = jnp.zeros((JS, RIM, LANES), jnp.float32)

time: 65.9 us -> 65.2 us (0.989)
  no operation moved by 1% of the time
where the time goes in v6:
time: 65.2 us; the launch traced here: 64.7 us
  Pallas kernels  64.1 us (98%)
    pallas_call x1, Pallas kernels, shards(): pl.pallas_call(functools.partial(kernel, (nsec, ngx, ngy, tile_y, strip_w...  61.7 us
    pallas_call x1, Pallas kernels, shards(): pl.pallas_call(write_results, out_shape=results, in_specs=[anywhere] * 5,...  2.44 us

profile of v6, /device:TPU:24, one launch (start us, length us, event | category | flops | bytes accessed | tf_op | source)
XLA Modules:
  0.0 64.7 jit_solution(6519067923669025871)
XLA Ops:
  0.6 61.7 %shard_map.128 = (f32[512,128]{1,0:T(8,128)}, f32[3,512,128]{2,1,0:T(8,128)}, f32[1,1,64,1024]{3,2,1,0:T(8,128)}, f32[8,8192]{1,0:T(8,128)}, f32[8,8192]{1,0:T(8,128)}) custom-call(f32[1,1,64,1024]{3,2,1,0:T(8,128)} %thick_in.1, s32[1,1,64,1024]{3,2,1,0:T(8,128)} %foot_in.1, f32[1,1,64,1024]{3,2,1,0:T(8,128)} %mom_in.1, f32[1,1,64,1024]{3,2,1,0:T(8,128)} %fric_in.1, ...), custom_call_target="tpu_custom_call" | custom-call | tf_op jit(solution)/shard_map/pallas_call | solution.py:657
  62.3 2.4 %shard_map.129 = (f32[512,128]{1,0:T(8,128)}, f32[3,512,128]{2,1,0:T(8,128)}, f32[1,1,64,1024]{3,2,1,0:T(8,128)}, f32[8,8192]{1,0:T(8,128)}, f32[8,8192]{1,0:T(8,128)}) custom-call(f32[512,128]{1,0:T(8,128)} %get-tuple-element.10.refs_0_, f32[3,512,128]{2,1,0:T(8,128)} %get-tuple-element.11.refs_1_, f32[1,1,64,1024]{3,2,1,0:T(8,128)} %get-tuple-element.12.refs_2_, ...), custom_call_target="tpu_custom_call" | custom-call | tf_op jit(solution)/shard_map/pallas_call | solution.py:708
